TPU v7x, 128 devices: a whole 4x4x4 slice. The times are simulated.
128 devices in a mesh: group: 4 (over x), shard: 32 (over y, z, core).
Axes of the slice: x: 4, y: 4, z: 4, core: 2. Of those that a mesh axis runs over, the one named last changes fastest.
Arguments:
- queries: float32 [1024, 768], P(('group', 'shard')), may hold values from -6 to 6
- codebook: float32 [96, 256, 8], replicated, may hold values from -0.21875 to 0.21875
- pq_codes: int32 [1024, 96, 256], P(('group', 'shard')), may hold values from 0 to 255
- probes: int32 [1024, 8], P('group'), may hold values from 0 to 255, all different within a row
- vectors: float32 [131072, 768], P(('group', 'shard')), may hold values from -0.21875 to 0.21875
- cand_owner: int32 [1024, 16], P(('group', 'shard')), may hold values from 0 to 127, all different within a row; in each aligned block of 8 rows (0 to 7, 8 to 15, ...) at most 2 rows name the same one
- cand_row: int32 [1024, 16], P(('group', 'shard')), may hold values from 0 to 1023
Outputs:
- pq_scores: float32 [1024, 256, 256], P(('group', 'shard'))
- rerank_scores: float32 [1024, 16], P(('group', 'shard'))
Inputs may be any that keep to these rules, and one draw needn't show every extreme that they name: The 8 probes of one query are distinct. `cand_owner`: the 16 owners of one query are distinct. Among the queries of one device no owner appears more than 2 times, and some owner appears exactly 2 times.
All inputs are finite; a program needn't handle non-finite values.
Results may differ from a plain program's by a relative error of at most 0.0029.
Values may be sent and summed in bfloat16 or wider, within the bound.
A program may use at most 128 MiB of HBM per device.

v0:
```python
import jax
import jax.numpy as jnp
from jax import lax
from jax.sharding import PartitionSpec as P

M = 96
DS = 8
KS = 256


def build_tables(query_rows, codebook):
    number = query_rows.shape[0]
    pieces = query_rows.reshape(number, M, DS)
    tables = jnp.einsum("qmd,mkd->qmk", pieces, codebook, precision=lax.Precision.HIGHEST)
    return tables.reshape(number, M * KS).astype(jnp.bfloat16)


def score_lists(pq_codes, group_tables, probes, first_list):
    centres = jnp.arange(KS, dtype=jnp.int32)

    def one_list(inputs):
        list_codes, list_id = inputs
        onehot = (list_codes[:, None, :] == centres[None, :, None]).astype(jnp.bfloat16)
        onehot = onehot.reshape(M * KS, list_codes.shape[1])
        scores = lax.dot_general(
            onehot, group_tables, (((0,), (1,)), ((), ())), preferred_element_type=jnp.float32
        )
        probed = jnp.any(probes == list_id, axis=1)
        return jnp.where(probed[None, :], scores, 0.0)

    list_ids = first_list + jnp.arange(pq_codes.shape[0], dtype=jnp.int32)
    return lax.map(one_list, (pq_codes, list_ids))


def rerank(queries, vectors, cand_owner, cand_row):
    owners = lax.axis_size("group") * lax.axis_size("shard")
    pair_count = cand_owner.shape[0] * cand_owner.shape[1]
    capacity = max(2, pair_count // owners)
    owner_flat = cand_owner.reshape(pair_count)
    matches = (owner_flat[:, None] == jnp.arange(owners, dtype=jnp.int32)[None, :]).astype(
        jnp.int32
    )
    before = jnp.cumsum(matches, axis=0) - matches
    position = jnp.sum(before * matches, axis=1)
    target = owner_flat * capacity + position
    source = jnp.arange(pair_count, dtype=jnp.int32) // cand_owner.shape[1]
    send_rows = (
        jnp.zeros((owners * capacity, queries.shape[1]), jnp.float32)
        .at[target]
        .set(queries[source])
    )
    send_rows = send_rows.reshape(owners, capacity, queries.shape[1])
    send_ids = (
        jnp.full((owners * capacity,), -1.0, jnp.float32)
        .at[target]
        .set(cand_row.reshape(pair_count).astype(jnp.float32))
    )
    send_ids = send_ids.reshape(owners, capacity)
    rows_in = lax.all_to_all(send_rows, ("group", "shard"), split_axis=0, concat_axis=0, tiled=True)
    row_ids = lax.all_to_all(send_ids, ("group", "shard"), split_axis=0, concat_axis=0, tiled=True)
    filled = row_ids >= 0.0
    lookup = jnp.maximum(row_ids, 0.0).astype(jnp.int32)
    found = vectors[lookup]
    inner = jnp.einsum("snd,snd->sn", rows_in, found, precision=lax.Precision.HIGHEST)
    scored = jnp.where(filled, inner, 0.0)
    returned = lax.all_to_all(scored, ("group", "shard"), split_axis=0, concat_axis=0, tiled=True)
    result = returned.reshape(owners * capacity)[target]
    return result.reshape(cand_owner.shape)


def per_device(queries, codebook, pq_codes, probes, vectors, cand_owner, cand_row):
    first_list = lax.axis_index("shard") * pq_codes.shape[0]
    own_tables = build_tables(queries, codebook)
    group_tables = lax.all_gather(own_tables, "shard", axis=0, tiled=True)
    pq_scores = score_lists(pq_codes, group_tables, probes, first_list)
    rerank_scores = rerank(queries, vectors, cand_owner, cand_row)
    return (pq_scores, rerank_scores)


def solution(mesh):
    in_specs = (
        P(("group", "shard"), None),
        P(),
        P(("group", "shard"), None, None),
        P("group", None),
        P(("group", "shard"), None),
        P(("group", "shard"), None),
        P(("group", "shard"), None),
    )
    out_specs = (P(("group", "shard"), None, None), P(("group", "shard"), None))
    return jax.shard_map(
        per_device, mesh=mesh, in_specs=in_specs, out_specs=out_specs, check_vma=False
    )
```

profile of v0, /device:TPU:1, one launch (start us, length us, event | category | flops | bytes accessed | tf_op | source)
XLA Modules:
  0.0 249.6 jit_solution(6174389318786089769)
XLA Ops:
  7.2 1.1 reshape.134
  8.4 2.9 %convolution_convert_fusion = bf16[96,256,8]{1,2,0:T(8,128)(2,1)} fusion(f32[96,256,8]{1,2,0:T(8,128)} %param.10, f32[8,96,8]{2,1,0:T(8,128)S(1)} %reshape.134), kind=kOutput, calls=%fused_computation.14 | convolution fusion | flops 19070976 | bytes 1204224 | tf_op jit(solution)/shard_map/qmd,mkd->qmk/dot_general | solution.py:14
  11.3 0.8 eq.43
  12.0 0.7 broadcast_multiply_fusion
  12.8 0.7 convert_element_type.36
  14.0 1.0 scatter_custom_fusion
  15.0 0.8 all_to_all.15
  15.8 11.5 %all-to-all-start = ((f32[128,1,2]{2,1,0:T(1,128)}), f32[128,1,2]{2,1,0:T(1,128)S(1)}, u32[]{:S(2)}, u32[]{:S(2)}) async-start(f32[128,1,2]{2,1,0:T(1,128)} %bitcast.4), calls=%async_computation | async-start | bytes 131072 | tf_op jit(solution)/shard_map/all_to_all | solution.py:60
  27.3 3.8 %scatter_custom_fusion.1 = f32[256,768]{1,0:T(8,128)} fusion(s32[128]{0:T(128)S(1)} %fusion.12, f32[8,768]{1,0:T(8,128)} %param.9, s32[1024]{0:T(1024)S(1)} %pad_clamp_fusion.2, f32[]{:T(128)} %constant.28.clone.1), kind=kCustom, calls=%fused_computation.17 | custom fusion | bytes 786944 | tf_op jit(solution)/shard_map/scatter | solution.py:50
  31.1 2.5 %reshape.135 = f32[128,2,768]{2,1,0:T(2,128)} reshape(f32[256,768]{1,0:T(8,128)} %scatter_custom_fusion.1) | data formatting | bytes 1572864 | tf_op jit(solution)/shard_map/reshape | solution.py:52
  33.6 3.0 %all-to-all-done = f32[128,1,2]{2,1,0:T(1,128)S(1)} async-done(((f32[128,1,2]{2,1,0:T(1,128)}), f32[128,1,2]{2,1,0:T(1,128)S(1)}, u32[]{:S(2)}, u32[]{:S(2)}) %all-to-all-start) | async-done | bytes 1056 | tf_op jit(solution)/shard_map/all_to_all | solution.py:60
  36.6 7.1 %all-to-all-start.1 = ((f32[128,2,768]{2,1,0:T(2,128)}), f32[128,2,768]{2,1,0:T(2,128)}, u32[]{:S(2)}, u32[]{:S(2)}) async-start(f32[128,2,768]{2,1,0:T(2,128)} %reshape.135), calls=%async_computation.1 | async-start | bytes 1572864 | tf_op jit(solution)/shard_map/all_to_all | solution.py:59
  44.2 2.0 gather_fusion
  46.1 2.6 %reshape.147 = f32[128,2,768]{2,1,0:T(2,128)} reshape(f32[256,768]{1,0:T(8,128)} %gather_fusion) | data formatting | bytes 1572864 | tf_op jit(solution)/shard_map/gather | solution.py:63
  48.7 11.2 %all-to-all-done.1 = f32[128,2,768]{2,1,0:T(2,128)} async-done(((f32[128,2,768]{2,1,0:T(2,128)}), f32[128,2,768]{2,1,0:T(2,128)}, u32[]{:S(2)}, u32[]{:S(2)}) %all-to-all-start.1) | async-done | bytes 786464 | tf_op jit(solution)/shard_map/all_to_all | solution.py:59
  60.0 1.9 multiply_reduce_fusion
  61.9 0.8 copy.22
  62.7 5.6 %all-to-all-start.2 = ((f32[128,1,2]{2,1,0:T(1,128)}), f32[128,1,2]{2,1,0:T(1,128)S(1)}, u32[]{:S(2)}, u32[]{:S(2)}) async-start(f32[128,1,2]{2,1,0:T(1,128)} %copy.22), calls=%async_computation.2 | async-start | bytes 131072 | tf_op jit(solution)/shard_map/all_to_all | solution.py:66
  68.3 9.3 %all-to-all-done.2 = f32[128,1,2]{2,1,0:T(1,128)S(1)} async-done(((f32[128,1,2]{2,1,0:T(1,128)}), f32[128,1,2]{2,1,0:T(1,128)S(1)}, u32[]{:S(2)}, u32[]{:S(2)}) %all-to-all-start.2) | async-done | bytes 1056 | tf_op jit(solution)/shard_map/all_to_all | solution.py:66
  78.2 0.8 reduce.5
  79.1 1.3 gather_fusion.1
  80.4 0.7 reshape.137
  81.1 4.4 %all-gather.2.cloned.1.call-done = bf16[256,24576]{1,0:T(8,128)(2,1)} async-done(((bf16[8,24576]{1,0:T(8,128)(2,1)}), bf16[256,24576]{1,0:T(8,128)(2,1)}) %all-gather.2.cloned.1.call-update) | async-done | bytes 12582928 | tf_op jit(solution)/shard_map/all_gather | solution.py:74
  85.4 157.4 %while.11 = (s32[]{:T(128)}, f32[8,256,256]{2,1,0:T(8,128)}, s32[8]{0:T(128)S(1)}, s32[256,8]{0,1:T(8,128)S(1)}, s32[8,96,256]{2,1,0:T(8,128)}, /*index=5*/bf16[256,24576]{1,0:T(8,128)(2,1)}, s32[]{:T(128)}) while((s32[]{:T(128)}, f32[8,256,256]{2,1,0:T(8,128)}, s32[8]{0:T(128)S(1)}, s32[256,8]{0,1:T(8,128)S(1)}, ...), condition=%wide.region_2.3_spmd.clone, body=%wide.region_0.2_spmd.clone.sunk | while | flops 3233877760 | bytes 38707820 | solution.py:32
  85.5 0.9 dynamic-slice_bitcast_fusion.2
  86.4 5.2 %fusion.24 = bf16[24576,256]{1,0:T(8,128)(2,1)} fusion(s32[24576]{0:T(1024)S(1)} %bitcast.55, s32[96,256]{1,0:T(8,128)S(1)} %dynamic-slice_bitcast_fusion.2), kind=kLoop, calls=%fused_computation.7.clone.1 | loop fusion | flops 12582912 | bytes 12779520 | tf_op jit(solution)/shard_map/while
  91.6 0.6 dynamic_slice.14
  92.2 0.6 compare_reduce_fusion.2
  92.8 12.3 %fusion.25 = f32[8,256,256]{2,1,0:T(8,128)} fusion(f32[8,256,256]{2,1,0:T(8,128)} %get-tuple-element.111, s32[]{:T(128)S(6)} %copy.36, bf16[24576,256]{1,0:T(8,128)(2,1)} %fusion.24, bf16[256,24576]{1,0:T(8,128)(2,1)} %get-tuple-element.122, pred[256]{0:T(512)(128)(4,1)S(1)} %compare_reduce_fusion.2), kind=kOutput, calls=%fused_computation.10.clone.1 | convolution fusion | flops 3221291008 | bytes 25428228 | tf_op jit(solution)/shard_map/while/body/eval_jaxpr/dot_general | solution.py:25
  105.2 0.9 dynamic-slice_bitcast_fusion.2
  106.1 5.2 %fusion.24 = bf16[24576,256]{1,0:T(8,128)(2,1)} fusion(s32[24576]{0:T(1024)S(1)} %bitcast.55, s32[96,256]{1,0:T(8,128)S(1)} %dynamic-slice_bitcast_fusion.2), kind=kLoop, calls=%fused_computation.7.clone.1 | loop fusion | flops 12582912 | bytes 12779520 | tf_op jit(solution)/shard_map/while
  111.3 0.6 dynamic_slice.14
  111.9 0.6 compare_reduce_fusion.2
  112.5 12.3 %fusion.25 = f32[8,256,256]{2,1,0:T(8,128)} fusion(f32[8,256,256]{2,1,0:T(8,128)} %get-tuple-element.111, s32[]{:T(128)S(6)} %copy.36, bf16[24576,256]{1,0:T(8,128)(2,1)} %fusion.24, bf16[256,24576]{1,0:T(8,128)(2,1)} %get-tuple-element.122, pred[256]{0:T(512)(128)(4,1)S(1)} %compare_reduce_fusion.2), kind=kOutput, calls=%fused_computation.10.clone.1 | convolution fusion | flops 3221291008 | bytes 25428228 | tf_op jit(solution)/shard_map/while/body/eval_jaxpr/dot_general | solution.py:25
  124.9 0.9 dynamic-slice_bitcast_fusion.2
  125.8 5.2 %fusion.24 = bf16[24576,256]{1,0:T(8,128)(2,1)} fusion(s32[24576]{0:T(1024)S(1)} %bitcast.55, s32[96,256]{1,0:T(8,128)S(1)} %dynamic-slice_bitcast_fusion.2), kind=kLoop, calls=%fused_computation.7.clone.1 | loop fusion | flops 12582912 | bytes 12779520 | tf_op jit(solution)/shard_map/while
  131.0 0.6 dynamic_slice.14
  131.5 0.6 compare_reduce_fusion.2
  132.1 12.3 %fusion.25 = f32[8,256,256]{2,1,0:T(8,128)} fusion(f32[8,256,256]{2,1,0:T(8,128)} %get-tuple-element.111, s32[]{:T(128)S(6)} %copy.36, bf16[24576,256]{1,0:T(8,128)(2,1)} %fusion.24, bf16[256,24576]{1,0:T(8,128)(2,1)} %get-tuple-element.122, pred[256]{0:T(512)(128)(4,1)S(1)} %compare_reduce_fusion.2), kind=kOutput, calls=%fused_computation.10.clone.1 | convolution fusion | flops 3221291008 | bytes 25428228 | tf_op jit(solution)/shard_map/while/body/eval_jaxpr/dot_general | solution.py:25
  144.5 0.9 dynamic-slice_bitcast_fusion.2
  145.4 5.2 %fusion.24 = bf16[24576,256]{1,0:T(8,128)(2,1)} fusion(s32[24576]{0:T(1024)S(1)} %bitcast.55, s32[96,256]{1,0:T(8,128)S(1)} %dynamic-slice_bitcast_fusion.2), kind=kLoop, calls=%fused_computation.7.clone.1 | loop fusion | flops 12582912 | bytes 12779520 | tf_op jit(solution)/shard_map/while
  150.6 0.6 dynamic_slice.14
  151.2 0.6 compare_reduce_fusion.2
  151.8 12.3 %fusion.25 = f32[8,256,256]{2,1,0:T(8,128)} fusion(f32[8,256,256]{2,1,0:T(8,128)} %get-tuple-element.111, s32[]{:T(128)S(6)} %copy.36, bf16[24576,256]{1,0:T(8,128)(2,1)} %fusion.24, bf16[256,24576]{1,0:T(8,128)(2,1)} %get-tuple-element.122, pred[256]{0:T(512)(128)(4,1)S(1)} %compare_reduce_fusion.2), kind=kOutput, calls=%fused_computation.10.clone.1 | convolution fusion | flops 3221291008 | bytes 25428228 | tf_op jit(solution)/shard_map/while/body/eval_jaxpr/dot_general | solution.py:25
  164.2 0.9 dynamic-slice_bitcast_fusion.2
  165.1 5.2 %fusion.24 = bf16[24576,256]{1,0:T(8,128)(2,1)} fusion(s32[24576]{0:T(1024)S(1)} %bitcast.55, s32[96,256]{1,0:T(8,128)S(1)} %dynamic-slice_bitcast_fusion.2), kind=kLoop, calls=%fused_computation.7.clone.1 | loop fusion | flops 12582912 | bytes 12779520 | tf_op jit(solution)/shard_map/while
  170.3 0.6 dynamic_slice.14
  170.9 0.6 compare_reduce_fusion.2
  171.5 12.3 %fusion.25 = f32[8,256,256]{2,1,0:T(8,128)} fusion(f32[8,256,256]{2,1,0:T(8,128)} %get-tuple-element.111, s32[]{:T(128)S(6)} %copy.36, bf16[24576,256]{1,0:T(8,128)(2,1)} %fusion.24, bf16[256,24576]{1,0:T(8,128)(2,1)} %get-tuple-element.122, pred[256]{0:T(512)(128)(4,1)S(1)} %compare_reduce_fusion.2), kind=kOutput, calls=%fused_computation.10.clone.1 | convolution fusion | flops 3221291008 | bytes 25428228 | tf_op jit(solution)/shard_map/while/body/eval_jaxpr/dot_general | solution.py:25
  183.9 0.9 dynamic-slice_bitcast_fusion.2
  184.8 5.2 %fusion.24 = bf16[24576,256]{1,0:T(8,128)(2,1)} fusion(s32[24576]{0:T(1024)S(1)} %bitcast.55, s32[96,256]{1,0:T(8,128)S(1)} %dynamic-slice_bitcast_fusion.2), kind=kLoop, calls=%fused_computation.7.clone.1 | loop fusion | flops 12582912 | bytes 12779520 | tf_op jit(solution)/shard_map/while
  190.0 0.6 dynamic_slice.14
  190.6 0.6 compare_reduce_fusion.2
  191.1 12.3 %fusion.25 = f32[8,256,256]{2,1,0:T(8,128)} fusion(f32[8,256,256]{2,1,0:T(8,128)} %get-tuple-element.111, s32[]{:T(128)S(6)} %copy.36, bf16[24576,256]{1,0:T(8,128)(2,1)} %fusion.24, bf16[256,24576]{1,0:T(8,128)(2,1)} %get-tuple-element.122, pred[256]{0:T(512)(128)(4,1)S(1)} %compare_reduce_fusion.2), kind=kOutput, calls=%fused_computation.10.clone.1 | convolution fusion | flops 3221291008 | bytes 25428228 | tf_op jit(solution)/shard_map/while/body/eval_jaxpr/dot_general | solution.py:25
  203.5 0.9 dynamic-slice_bitcast_fusion.2
  204.4 5.2 %fusion.24 = bf16[24576,256]{1,0:T(8,128)(2,1)} fusion(s32[24576]{0:T(1024)S(1)} %bitcast.55, s32[96,256]{1,0:T(8,128)S(1)} %dynamic-slice_bitcast_fusion.2), kind=kLoop, calls=%fused_computation.7.clone.1 | loop fusion | flops 12582912 | bytes 12779520 | tf_op jit(solution)/shard_map/while
  209.6 0.6 dynamic_slice.14
  210.2 0.6 compare_reduce_fusion.2
  210.8 12.3 %fusion.25 = f32[8,256,256]{2,1,0:T(8,128)} fusion(f32[8,256,256]{2,1,0:T(8,128)} %get-tuple-element.111, s32[]{:T(128)S(6)} %copy.36, bf16[24576,256]{1,0:T(8,128)(2,1)} %fusion.24, bf16[256,24576]{1,0:T(8,128)(2,1)} %get-tuple-element.122, pred[256]{0:T(512)(128)(4,1)S(1)} %compare_reduce_fusion.2), kind=kOutput, calls=%fused_computation.10.clone.1 | convolution fusion | flops 3221291008 | bytes 25428228 | tf_op jit(solution)/shard_map/while/body/eval_jaxpr/dot_general | solution.py:25
  223.2 0.9 dynamic-slice_bitcast_fusion.2
  224.1 5.2 %fusion.24 = bf16[24576,256]{1,0:T(8,128)(2,1)} fusion(s32[24576]{0:T(1024)S(1)} %bitcast.55, s32[96,256]{1,0:T(8,128)S(1)} %dynamic-slice_bitcast_fusion.2), kind=kLoop, calls=%fused_computation.7.clone.1 | loop fusion | flops 12582912 | bytes 12779520 | tf_op jit(solution)/shard_map/while
  229.3 0.6 dynamic_slice.14
  229.9 0.6 compare_reduce_fusion.2
  230.5 12.3 %fusion.25 = f32[8,256,256]{2,1,0:T(8,128)} fusion(f32[8,256,256]{2,1,0:T(8,128)} %get-tuple-element.111, s32[]{:T(128)S(6)} %copy.36, bf16[24576,256]{1,0:T(8,128)(2,1)} %fusion.24, bf16[256,24576]{1,0:T(8,128)(2,1)} %get-tuple-element.122, pred[256]{0:T(512)(128)(4,1)S(1)} %compare_reduce_fusion.2), kind=kOutput, calls=%fused_computation.10.clone.1 | convolution fusion | flops 3221291008 | bytes 25428228 | tf_op jit(solution)/shard_map/while/body/eval_jaxpr/dot_general | solution.py:25
  (42 shorter events, 2.2 us)
Async XLA Ops:
  7.2 37.0 %copy-start = (f32[1024,768]{1,0:T(8,128)S(1)}, f32[1024,768]{1,0:T(8,128)}, u32[]{:S(2)}) copy-start(f32[1024,768]{1,0:T(8,128)} %param.13) | copy-start | bytes 9437188
  7.2 78.3 %copy-start.1 = (s32[256,8]{0,1:T(8,128)S(1)}, s32[256,8]{0,1:T(8,128)}, u32[]{:S(2)}) copy-start(s32[256,8]{0,1:T(8,128)} %param.12) | copy-start | bytes 24580
  7.2 78.3 %all-gather.2.cloned.1.call-start = ((), (), s32[]{:S(2)}) async-start(), calls=%async_computation.3 | async-start | bytes 12976128 | tf_op jit(solution)/shard_map/all_gather | solution.py:74
  15.8 20.9 %all-to-all-start = ((f32[128,1,2]{2,1,0:T(1,128)}), f32[128,1,2]{2,1,0:T(1,128)S(1)}, u32[]{:S(2)}, u32[]{:S(2)}) async-start(f32[128,1,2]{2,1,0:T(1,128)} %bitcast.4), calls=%async_computation | async-start | bytes 131072 | tf_op jit(solution)/shard_map/all_to_all | solution.py:60
  36.6 23.3 %all-to-all-start.1 = ((f32[128,2,768]{2,1,0:T(2,128)}), f32[128,2,768]{2,1,0:T(2,128)}, u32[]{:S(2)}, u32[]{:S(2)}) async-start(f32[128,2,768]{2,1,0:T(2,128)} %reshape.135), calls=%async_computation.1 | async-start | bytes 1572864 | tf_op jit(solution)/shard_map/all_to_all | solution.py:59
  62.7 15.0 %all-to-all-start.2 = ((f32[128,1,2]{2,1,0:T(1,128)}), f32[128,1,2]{2,1,0:T(1,128)S(1)}, u32[]{:S(2)}, u32[]{:S(2)}) async-start(f32[128,1,2]{2,1,0:T(1,128)} %copy.22), calls=%async_computation.2 | async-start | bytes 131072 | tf_op jit(solution)/shard_map/all_to_all | solution.py:66
Sparse Core Ops, SparseCore 0:
  11.4 74.0 all-gather.1
where the time goes:
time: 250 us
  matrix products  102 us (41%)
  other arithmetic  50.8 us (20%)
  local copies, waits for them, and re-layouts  30.7 us (12%)
  waiting for transfers between devices  28 us (11%)
  starting transfers between devices  24.3 us (10%)
  between operations  14.2 us (6%)
    dot_general x8, matrix products, one_list(): lax.dot_general(onehot, group_tables, (((0,), (1,)), ((), ())), preferred...  98.7 us
    while x8, other arithmetic  41.6 us
    all_to_all x1, starting transfers between devices, rerank(): lax.all_to_all(send_ids, ('group', 'shard'), split_axis=0, concat_axis=0,...  11.5 us
    all_to_all x1, waiting for transfers between devices, rerank(): lax.all_to_all(send_rows, ('group', 'shard'), split_axis=0, concat_axis=0...  11.2 us
    all_to_all x1, waiting for transfers between devices, rerank(): lax.all_to_all(scored, ('group', 'shard'), split_axis=0, concat_axis=0, t...  9.34 us
    eq x8, local copies, waits for them, and re-layouts, one_list(): list_codes[:, None, :] == centres[None, :, None]  7.25 us
    all_to_all x1, starting transfers between devices, rerank(): lax.all_to_all(send_rows, ('group', 'shard'), split_axis=0, concat_axis=0...  7.13 us
    all_to_all x1, starting transfers between devices, rerank(): lax.all_to_all(scored, ('group', 'shard'), split_axis=0, concat_axis=0, t...  5.63 us
  transfers between devices with their start and end apart: 4, of which 4 were waited for; matrix products, arithmetic and copies ran while one was open for 8% of the time, Pallas kernels for 0%

commit v1 on v0

v1 whole, which is shorter than its diff:
```python
import jax
import jax.numpy as jnp
from jax import lax
from jax.experimental import pallas as pl
from jax.experimental.pallas import tpu as pltpu
from jax.sharding import PartitionSpec as P

MESH = pl.DeviceIdType.MESH
F32, BF16, I32 = jnp.float32, jnp.bfloat16, jnp.int32


def lane_gather(table, index):
    numbers = lax.GatherDimensionNumbers(
        offset_dims=(),
        collapsed_slice_dims=(1,),
        start_index_map=(1,),
        operand_batching_dims=(0,),
        start_indices_batching_dims=(0,),
    )
    return lax.gather(
        table, index[..., None], numbers, (1, 1), mode=lax.GatherScatterMode.PROMISE_IN_BOUNDS
    )


def iota(shape, dim):
    return lax.broadcasted_iota(I32, shape, dim)


def kernel(
    q_ref,
    probes_ref,
    owner_ref,
    row_ref,
    codes_hbm,
    book_hbm,
    vectors_hbm,
    pq_ref,
    rr_ref,
    codes,
    book,
    vectors,
    book16,
    vectors16,
    decoded,
    group_q,
    cube_q,
    cube_want,
    want_t,
    want_out,
    want_in,
    slot_out,
    slot_in,
    score_out,
    score_in,
    spread,
    back,
    total,
    load_sem,
    cq_s, cq_r, cw_s, cw_r,
    g_s, g_r,
    sq_s, sq_r, sw_s, sw_r,
    rs_s, rs_r, bk_s, bk_r,
):
    x = lax.axis_index("group")
    s = lax.axis_index("shard")
    y, z, c = s // 8, (s // 2) % 4, s % 2
    a = x * 2 + c
    w = y * 4 + z

    def device(x, y, z, c):
        return {"group": x, "shard": (y * 4 + z) * 2 + c}

    def cube_peer(i):
        p = (a + i) % 8
        return p, device(p // 2, y, z, p % 2)

    def plane_peer(i):
        p = (w + i) % 16
        return p, device(x, p // 4, p % 4, c)

    loads = [
        pltpu.make_async_copy(src, dst, load_sem.at[i])
        for i, (src, dst) in enumerate(
            ((book_hbm, book), (codes_hbm, codes), (vectors_hbm, vectors))
        )
    ]
    for load in loads:
        load.start()

    barrier = pltpu.get_barrier_semaphore()
    for i in range(1, 8):
        pl.semaphore_signal(barrier, inc=1, device_id=cube_peer(i)[1], device_id_type=MESH)
    for i in range(1, 16):
        pl.semaphore_signal(barrier, inc=1, device_id=plane_peer(i)[1], device_id_type=MESH)

    def remote(src, dst, send, recv, to):
        return pltpu.make_async_remote_copy(
            src_ref=src, dst_ref=dst, send_sem=send, recv_sem=recv, device_id=to, device_id_type=MESH
        )

    q = q_ref[...]
    high = q.astype(BF16)
    low = (q - high.astype(F32)).astype(BF16)
    cube_q[a] = jnp.concatenate([high[:, :384], high[:, 384:]], axis=0)
    for h in range(2):
        group_q[h, y, z, c] = jnp.concatenate(
            [high[:, h * 384 : h * 384 + 384], low[:, h * 384 : h * 384 + 384]], axis=0
        )
    owner = owner_ref[...]
    row = row_ref[...].astype(F32)
    lanes = iota((8, 128), 1)
    present = jnp.zeros((8, 128), F32)
    wanted = jnp.zeros((8, 128), F32)
    for k in range(16):
        hit = owner[:, k : k + 1] == lanes
        present = jnp.where(hit, 1.0, present)
        wanted = jnp.where(hit, row[:, k : k + 1], wanted)
    earlier = (iota((8, 8), 1) < iota((8, 8), 0)).astype(BF16)
    rank = jnp.dot(earlier, present.astype(BF16), preferred_element_type=F32)
    slot = (a * 2).astype(F32) + rank
    cube_want[a] = jnp.where(present > 0.0, slot * 1024.0 + wanted, -1.0)
    spread[...] = jnp.zeros((128, 128), F32)

    pl.semaphore_wait(barrier, 22)

    cube_copies = []
    for i in range(1, 8):
        _, to = cube_peer(i)
        for copy in (
            remote(cube_q.at[a], cube_q.at[a], cq_s.at[i], cq_r.at[i], to),
            remote(cube_want.at[a], cube_want.at[a], cw_s.at[i], cw_r.at[i], to),
        ):
            copy.start()
            cube_copies.append(copy)

    def line_peer(axis, i):
        return (
            device(x, (y + i) % 4, z, c) if axis == 0 else device(x, y, (z + i) % 4, c)
        )

    first_copies, second_copies = [], []
    for i in (1, 3, 2):
        for h in range(2):
            block = group_q.at[h, y, z, c]
            copy = remote(block, block, g_s.at[h, 0, i], g_r.at[h, 0, i], line_peer(h, i))
            copy.start()
            first_copies.append(copy)

    loads[0].wait()

    def to_book16(i, _):
        pair = book[pl.ds(i * 2, 2)]
        book16[i] = jnp.concatenate([pair[0], pair[1]], axis=0).astype(BF16)
        return 0

    lax.fori_loop(0, 48, to_book16, 0, unroll=8)
    loads[1].wait()

    def decode(l, _):
        for m in range(48):
            for h in range(2):
                span = slice(h * 128, h * 128 + 128)
                index = jnp.concatenate(
                    [
                        jnp.broadcast_to(codes[l, 2 * m : 2 * m + 1, span], (8, 128)),
                        jnp.broadcast_to(codes[l, 2 * m + 1 : 2 * m + 2, span], (8, 128)),
                    ],
                    axis=0,
                )
                near = (index & 127).astype(jnp.int16)
                decoded[l, m * 16 : m * 16 + 16, span] = jnp.where(
                    index < 128,
                    lane_gather(book16[m, :, :128], near),
                    lane_gather(book16[m, :, 128:], near),
                )
        return 0

    lax.fori_loop(0, 2, decode, 0)

    for copy in cube_copies:
        copy.wait_recv()
    wants = jnp.concatenate(
        [cube_want[...].reshape(64, 128), jnp.full((64, 128), -1.0, F32)], axis=0
    )
    want_t[...] = wants.T.astype(I32)
    places = iota((16, 128), 0)
    picks = []
    for p in range(16):
        line = want_t[pl.ds(x * 32 + p * 2 + c, 1), :]
        want_out[p] = line
        picks.append(
            jnp.where((jnp.broadcast_to(line, (16, 128)) >> 10) == places, 1.0, 0.0)
        )
    pick = jnp.concatenate(picks, axis=0)[:, :64].astype(BF16)
    cube = cube_q[...]
    for h in range(2):
        columns = cube[:, h * 8 : h * 8 + 8, :].reshape(64, 384)
        chosen = jnp.dot(pick, columns, preferred_element_type=F32).astype(BF16)
        slot_out[:, :, h * 384 : h * 384 + 384] = chosen.reshape(16, 16, 384)
    slot_in[w] = slot_out[w]
    want_in[w] = want_out[w]
    slot_copies = []
    for i in range(1, 16):
        p, to = plane_peer(i)
        for copy in (
            remote(slot_out.at[p], slot_in.at[w], sq_s.at[i], sq_r.at[i], to),
            remote(want_out.at[p], want_in.at[w], sw_s.at[i], sw_r.at[i], to),
        ):
            copy.start()
            slot_copies.append(copy)

    for copy in first_copies:
        copy.wait_recv()
    for i in (1, 3, 2):
        for h in range(2):
            block = group_q.at[h, :, z, c] if h == 0 else group_q.at[h, y, :, c]
            copy = remote(block, block, g_s.at[h, 1, i], g_r.at[h, 1, i], line_peer(1 - h, i))
            copy.start()
            second_copies.append(copy)

    lax.fori_loop(2, 5, decode, 0)
    loads[2].wait()

    def to_vectors16(i, _):
        span = pl.ds(pl.multiple_of(i * 128, 128), 128)
        vectors16[span, :] = vectors[span, :].astype(BF16)
        return 0

    lax.fori_loop(0, 8, to_vectors16, 0)

    for copy in second_copies:
        copy.wait_recv()
    sibling = device(x, y, z, 1 - c)
    core_copies = []
    for h in range(2):
        block = group_q.at[h, :, :, c]
        copy = remote(block, block, g_s.at[h, 2, 0], g_r.at[h, 2, 0], sibling)
        copy.start()
        core_copies.append(copy)

    lax.fori_loop(5, 8, decode, 0)

    for copy in slot_copies:
        copy.wait_recv()
    slots = slot_in[...].reshape(256, 768)
    ids = []
    for p in range(16):
        line = jnp.broadcast_to(want_in[p], (16, 128))
        ids.append(jnp.where((line >> 10) == places, line & 1023, 0))
    ids = jnp.sum(jnp.concatenate(ids, axis=0).astype(F32), axis=1, keepdims=True).astype(I32)
    found = jnp.zeros((256, 256), F32)
    for b in range(4):
        part = lax.dot_general(
            slots,
            vectors16[b * 256 : b * 256 + 256, :],
            (((1,), (1,)), ((), ())),
            preferred_element_type=F32,
        )
        found = jnp.where(iota((256, 256), 1) + b * 256 == ids, part, found)
        if b == 0:
            found = jnp.where(iota((256, 256), 1) == ids, part, 0.0)
    scored = jnp.sum(found, axis=1, keepdims=True)
    for p in range(16):
        mine = jnp.broadcast_to(scored[p * 16 : p * 16 + 16, :], (16, 128))
        score_out[p] = jnp.sum(
            jnp.where(iota((16, 128), 1) == places, mine, 0.0), axis=0, keepdims=True
        )
    score_in[w] = score_out[w]
    score_copies = []
    for i in range(1, 16):
        p, to = plane_peer(i)
        copy = remote(score_out.at[p], score_in.at[w], rs_s.at[i], rs_r.at[i], to)
        copy.start()
        score_copies.append(copy)

    for copy in core_copies:
        copy.wait_recv()

    probes = probes_ref[...]

    def score_list(l, _):
        left = jnp.concatenate(
            [group_q[0].reshape(512, 384), group_q[1].reshape(512, 384)], axis=1
        )
        both = jnp.dot(left, decoded[l], preferred_element_type=F32).reshape(32, 2, 8, 256)
        sums = (both[:, 0] + both[:, 1]).reshape(256, 256)
        probed = jnp.max(jnp.where(probes == s * 8 + l, 1.0, 0.0), axis=0, keepdims=True)
        pq_ref[l] = jnp.where(probed > 0.0, sums.T, 0.0)
        return 0

    lax.fori_loop(0, 4, score_list, 0)

    for copy in score_copies:
        copy.wait_recv()
    for p in range(16):
        spread[pl.ds(x * 32 + p * 2 + c, 1), :] = score_in[p]
    back[a] = spread[...].T[:16, :]
    back_copies = []
    for i in range(1, 8):
        _, to = cube_peer(i)
        copy = remote(back.at[a], back.at[a], bk_s.at[i], bk_r.at[i], to)
        copy.start()
        back_copies.append(copy)

    lax.fori_loop(4, 8, score_list, 0)

    for copy in back_copies:
        copy.wait_recv()
    total[...] = jnp.sum(back[...], axis=0)
    own = jnp.where(rank < 0.5, total[pl.ds(a * 2, 1), :], total[pl.ds(a * 2 + 1, 1), :])
    result = jnp.zeros((8, 16), F32)
    for k in range(16):
        value = jnp.sum(
            jnp.where(owner[:, k : k + 1] == lanes, own, 0.0), axis=1, keepdims=True
        )
        result = jnp.where(iota((8, 16), 1) == k, value, result)
    rr_ref[...] = result

    for copy in (
        cube_copies + first_copies + second_copies + core_copies
        + slot_copies + score_copies + back_copies
    ):
        copy.wait_send()


def per_device(queries, codebook, pq_codes, probes, vectors, cand_owner, cand_row):
    vmem = pl.BlockSpec(memory_space=pltpu.VMEM)
    hbm = pl.BlockSpec(memory_space=pl.ANY)
    dma = pltpu.SemaphoreType.DMA
    return pl.pallas_call(
        kernel,
        out_shape=(
            jax.ShapeDtypeStruct((8, 256, 256), F32),
            jax.ShapeDtypeStruct((8, 16), F32),
        ),
        in_specs=[vmem] * 4 + [hbm] * 3,
        out_specs=(vmem, vmem),
        scratch_shapes=[
            pltpu.VMEM((8, 96, 256), I32),
            pltpu.VMEM((96, 8, 256), F32),
            pltpu.VMEM((1024, 768), F32),
            pltpu.VMEM((48, 16, 256), BF16),
            pltpu.VMEM((1024, 768), BF16),
            pltpu.VMEM((8, 768, 256), BF16),
            pltpu.VMEM((2, 4, 4, 2, 16, 384), BF16),
            pltpu.VMEM((8, 16, 384), BF16),
            pltpu.VMEM((8, 8, 128), F32),
            pltpu.VMEM((128, 128), I32),
            pltpu.VMEM((16, 1, 128), I32),
            pltpu.VMEM((16, 1, 128), I32),
            pltpu.VMEM((16, 16, 768), BF16),
            pltpu.VMEM((16, 16, 768), BF16),
            pltpu.VMEM((16, 1, 128), F32),
            pltpu.VMEM((16, 1, 128), F32),
            pltpu.VMEM((128, 128), F32),
            pltpu.VMEM((8, 16, 128), F32),
            pltpu.VMEM((16, 128), F32),
            dma((3,)),
            dma((8,)), dma((8,)), dma((8,)), dma((8,)),
            dma((2, 3, 4)), dma((2, 3, 4)),
            dma((16,)), dma((16,)), dma((16,)), dma((16,)),
            dma((16,)), dma((16,)), dma((8,)), dma((8,)),
        ],
        compiler_params=pltpu.CompilerParams(
            vmem_limit_bytes=48 << 20, collective_id=0, has_side_effects=True
        ),
        cost_estimate=pl.CostEstimate(flops=3_000_000_000, bytes_accessed=7_000_000, transcendentals=0),
        name="search",
    )(
        queries,
        probes.T,
        cand_owner,
        cand_row,
        pq_codes,
        codebook.transpose(0, 2, 1),
        vectors,
    )


def solution(mesh):
    both = ("group", "shard")
    in_specs = (
        P(both, None),
        P(),
        P(both, None, None),
        P("group", None),
        P(both, None),
        P(both, None),
        P(both, None),
    )
    out_specs = (P(both, None, None), P(both, None))
    return jax.shard_map(
        per_device, mesh=mesh, in_specs=in_specs, out_specs=out_specs, check_vma=False
    )
```

time: 250 us -> 42.8 us (0.17)
  matrix products: 102 us -> 0 us
  other arithmetic: 50.8 us -> 0 us
  Pallas kernels: 0 us -> 34.8 us
  waiting for transfers between devices: 28 us -> 0 us
  starting transfers between devices: 24.3 us -> 0 us
  local copies, waits for them, and re-layouts: 30.7 us -> 6.98 us
  between operations: 14.2 us -> 0.65 us
    dot_general x9 -> x0, matrix products: 102 us -> none  [the longest x8 98.7 us: one_list(): lax.dot_general(onehot, group_tables, (((0,), (1,)), ((), ())), preferred...]
    while x8 -> x0, other arithmetic: 41.6 us -> none
    pallas_call x0 -> x1, Pallas kernels: none -> 34.8 us  [per_device(): pl.pallas_call(kernel, out_shape=(jax.ShapeDtypeStruct((8, 256, 256), F32...]
    all_to_all x3 -> x0, starting transfers between devices: 24.3 us -> none  [the longest x1 11.5 us: rerank(): lax.all_to_all(send_ids, ('group', 'shard'), split_axis=0, concat_axis=0,...]
    all_to_all x3 -> x0, waiting for transfers between devices: 23.6 us -> none  [the longest x1 11.2 us: rerank(): lax.all_to_all(send_rows, ('group', 'shard'), split_axis=0, concat_axis=0...]
    eq x9 -> x0, local copies, waits for them, and re-layouts: 8.01 us -> none  [the longest x8 7.25 us: one_list(): list_codes[:, None, :] == centres[None, :, None]]
    unnamed x4 -> x14, local copies, waits for them, and re-layouts: 0.01 us -> 6.98 us
    gather x3 -> x0, local copies, waits for them, and re-layouts: 5.83 us -> none  [the longest x2 4.56 us: rerank(): found = vectors[lookup]]
  transfers between devices with their start and end apart: 4 -> 0, of which waited for: 4 -> 0; matrix products, arithmetic and copies ran while one was open for 8% -> 0% of each run, Pallas kernels for 0% -> 0%
where the time goes in v1:
time: 42.8 us; the launch traced here: 42.5 us
  Pallas kernels  34.8 us (81%)
  local copies, waits for them, and re-layouts  6.98 us (16%)
  between operations  0.65 us (2%)
    pallas_call x1, Pallas kernels, per_device(): pl.pallas_call(kernel, out_shape=(jax.ShapeDtypeStruct((8, 256, 256), F32...  34.8 us
    unnamed x14, local copies, waits for them, and re-layouts  6.98 us

profile of v1, /device:TPU:1, one launch (start us, length us, event | category | flops | bytes accessed | tf_op | source)
XLA Modules:
  0.0 42.5 jit_solution(18080436496093085879)
XLA Ops:
  0.6 0.0 copy-start
  0.6 1.1 %copy-done = s32[8,96,256]{2,1,0:T(8,128)S(1)} copy-done((s32[8,96,256]{2,1,0:T(8,128)S(1)}, s32[8,96,256]{2,1,0:T(8,128)}, u32[]{:S(2)}) %copy-start) | copy-done | bytes 786456
  1.8 0.0 copy-start.1
  1.8 1.1 %copy-done.1 = f32[96,256,8]{1,2,0:T(8,128)S(1)} copy-done((f32[96,256,8]{1,2,0:T(8,128)S(1)}, f32[96,256,8]{1,2,0:T(8,128)}, u32[]{:S(2)}) %copy-start.1) | copy-done | bytes 786456
  2.9 0.0 copy-start.2
  2.9 0.7 %copy-done.2 = f32[8,768]{1,0:T(8,128)S(1)} copy-done((f32[8,768]{1,0:T(8,128)S(1)}, f32[8,768]{1,0:T(8,128)}, u32[]{:S(2)}) %copy-start.2) | copy-done | bytes 24600
  3.6 0.0 copy-start.3
  3.6 0.7 %copy-done.3 = s32[256,8]{0,1:T(8,128)S(1)} copy-done((s32[256,8]{0,1:T(8,128)S(1)}, s32[256,8]{0,1:T(8,128)}, u32[]{:S(2)}) %copy-start.3) | copy-done | bytes 8216
  4.3 0.0 copy-start.4
  4.3 0.7 %copy-done.4 = s32[8,16]{1,0:T(8,128)S(1)} copy-done((s32[8,16]{1,0:T(8,128)S(1)}, s32[8,16]{1,0:T(8,128)}, u32[]{:S(2)}) %copy-start.4) | copy-done | bytes 536
  5.0 0.0 copy-start.5
  5.0 0.7 %copy-done.5 = s32[8,16]{1,0:T(8,128)S(1)} copy-done((s32[8,16]{1,0:T(8,128)S(1)}, s32[8,16]{1,0:T(8,128)}, u32[]{:S(2)}) %copy-start.5) | copy-done | bytes 536
  5.7 34.8 %search.1 = (f32[8,256,256]{2,1,0:T(8,128)S(1)}, f32[8,16]{1,0:T(8,128)S(1)}) custom-call(f32[8,768]{1,0:T(8,128)S(1)} %copy-done.2, s32[8,256]{1,0:T(8,128)S(1)} %bitcast.3, s32[8,16]{1,0:T(8,128)S(1)} %copy-done.4, s32[8,16]{1,0:T(8,128)S(1)} %copy-done.5, s32[8,96,256]{2,1,0:T(8,128)S(1)} %copy-done, f32[96,8,256]{2,1,0:T(8,128)S(1)} %bitcast.2, ...), custom_call_target="tpu_custom_call" | custom-call | flops 3000000000 | bytes 7000000 | tf_op jit(solution)/shard_map/search/pallas_call | solution.py:330
  40.6 1.3 %copy.11 = f32[8,256,256]{2,1,0:T(8,128)} copy(f32[8,256,256]{2,1,0:T(8,128)S(1)} %get-tuple-element.4) | data formatting | bytes 4194304
  41.9 0.6 %copy.12 = f32[8,16]{1,0:T(8,128)} copy(f32[8,16]{1,0:T(8,128)S(1)} %get-tuple-element.5) | data formatting | bytes 1024
Async XLA Ops:
  0.6 1.1 %copy-start = (s32[8,96,256]{2,1,0:T(8,128)S(1)}, s32[8,96,256]{2,1,0:T(8,128)}, u32[]{:S(2)}) copy-start(s32[8,96,256]{2,1,0:T(8,128)} %codes_hbm.1) | copy-start | bytes 2359300
  1.8 1.1 %copy-start.1 = (f32[96,256,8]{1,2,0:T(8,128)S(1)}, f32[96,256,8]{1,2,0:T(8,128)}, u32[]{:S(2)}) copy-start(f32[96,256,8]{1,2,0:T(8,128)} %param.8) | copy-start | bytes 2359300
  2.9 0.7 %copy-start.2 = (f32[8,768]{1,0:T(8,128)S(1)}, f32[8,768]{1,0:T(8,128)}, u32[]{:S(2)}) copy-start(f32[8,768]{1,0:T(8,128)} %q_ref.1) | copy-start | bytes 73732
  3.6 0.7 %copy-start.3 = (s32[256,8]{0,1:T(8,128)S(1)}, s32[256,8]{0,1:T(8,128)}, u32[]{:S(2)}) copy-start(s32[256,8]{0,1:T(8,128)} %param.10) | copy-start | bytes 24580
  4.3 0.7 %copy-start.4 = (s32[8,16]{1,0:T(8,128)S(1)}, s32[8,16]{1,0:T(8,128)}, u32[]{:S(2)}) copy-start(s32[8,16]{1,0:T(8,128)} %owner_ref.1) | copy-start | bytes 1540
  5.0 0.7 %copy-start.5 = (s32[8,16]{1,0:T(8,128)S(1)}, s32[8,16]{1,0:T(8,128)}, u32[]{:S(2)}) copy-start(s32[8,16]{1,0:T(8,128)} %row_ref.1) | copy-start | bytes 1540

commit v2 on v1

--- a/solution.py
+++ b/solution.py
@@ -27,15 +27,19 @@
 
 
 def kernel(
-    q_ref,
-    probes_ref,
-    owner_ref,
-    row_ref,
+    q_hbm,
+    probes_hbm,
+    owner_hbm,
+    row_hbm,
     codes_hbm,
     book_hbm,
     vectors_hbm,
     pq_ref,
     rr_ref,
+    q_ref,
+    probes_ref,
+    owner_ref,
+    row_ref,
     codes,
     book,
     vectors,
@@ -44,7 +48,6 @@
     decoded,
     group_q,
     cube_q,
-    cube_want,
     want_t,
     want_out,
     want_in,
@@ -52,18 +55,17 @@
     slot_in,
     score_out,
     score_in,
-    spread,
-    back,
     total,
     load_sem,
-    cq_s, cq_r, cw_s, cw_r,
+    cq_s, cq_r,
     g_s, g_r,
     sq_s, sq_r, sw_s, sw_r,
-    rs_s, rs_r, bk_s, bk_r,
+    rs_s, rs_r,
 ):
     x = lax.axis_index("group")
     s = lax.axis_index("shard")
     y, z, c = s // 8, (s // 2) % 4, s % 2
+    me = x * 32 + s
     a = x * 2 + c
     w = y * 4 + z
 
@@ -81,7 +83,15 @@
     loads = [
         pltpu.make_async_copy(src, dst, load_sem.at[i])
         for i, (src, dst) in enumerate(
-            ((book_hbm, book), (codes_hbm, codes), (vectors_hbm, vectors))
+            (
+                (q_hbm, q_ref),
+                (owner_hbm, owner_ref),
+                (row_hbm, row_ref),
+                (book_hbm, book),
+                (codes_hbm, codes),
+                (probes_hbm, probes_ref),
+                (vectors_hbm, vectors),
+            )
         )
     ]
     for load in loads:
@@ -98,10 +108,12 @@
             src_ref=src, dst_ref=dst, send_sem=send, recv_sem=recv, device_id=to, device_id_type=MESH
         )
 
+    for load in loads[:3]:
+        load.wait()
     q = q_ref[...]
     high = q.astype(BF16)
     low = (q - high.astype(F32)).astype(BF16)
-    cube_q[a] = jnp.concatenate([high[:, :384], high[:, 384:]], axis=0)
+    cube_q[a, :, :384] = jnp.concatenate([high[:, :384], high[:, 384:]], axis=0)
     for h in range(2):
         group_q[h, y, z, c] = jnp.concatenate(
             [high[:, h * 384 : h * 384 + 384], low[:, h * 384 : h * 384 + 384]], axis=0
@@ -118,20 +130,19 @@
     earlier = (iota((8, 8), 1) < iota((8, 8), 0)).astype(BF16)
     rank = jnp.dot(earlier, present.astype(BF16), preferred_element_type=F32)
     slot = (a * 2).astype(F32) + rank
-    cube_want[a] = jnp.where(present > 0.0, slot * 1024.0 + wanted, -1.0)
-    spread[...] = jnp.zeros((128, 128), F32)
+    upper = jnp.floor(wanted * (1.0 / 128.0))
+    cube_q[a, :, 384:] = jnp.concatenate(
+        [jnp.where(present > 0.0, slot * 8.0 + upper, -1.0), wanted - upper * 128.0], axis=0
+    ).astype(BF16)
 
     pl.semaphore_wait(barrier, 22)
 
     cube_copies = []
     for i in range(1, 8):
         _, to = cube_peer(i)
-        for copy in (
-            remote(cube_q.at[a], cube_q.at[a], cq_s.at[i], cq_r.at[i], to),
-            remote(cube_want.at[a], cube_want.at[a], cw_s.at[i], cw_r.at[i], to),
-        ):
-            copy.start()
-            cube_copies.append(copy)
+        copy = remote(cube_q.at[a], cube_q.at[a], cq_s.at[i], cq_r.at[i], to)
+        copy.start()
+        cube_copies.append(copy)
 
     def line_peer(axis, i):
         return (
@@ -146,7 +157,7 @@
             copy.start()
             first_copies.append(copy)
 
-    loads[0].wait()
+    loads[3].wait()
 
     def to_book16(i, _):
         pair = book[pl.ds(i * 2, 2)]
@@ -154,7 +165,7 @@
         return 0
 
     lax.fori_loop(0, 48, to_book16, 0, unroll=8)
-    loads[1].wait()
+    loads[4].wait()
 
     def decode(l, _):
         for m in range(48):
@@ -179,9 +190,10 @@
 
     for copy in cube_copies:
         copy.wait_recv()
-    wants = jnp.concatenate(
-        [cube_want[...].reshape(64, 128), jnp.full((64, 128), -1.0, F32)], axis=0
-    )
+    cube = cube_q[...]
+    digits = cube[:, :, 384:].astype(F32)
+    wants = (digits[:, :8] * 128.0 + digits[:, 8:]).reshape(64, 128)
+    wants = jnp.concatenate([wants, jnp.full((64, 128), -1.0, F32)], axis=0)
     want_t[...] = wants.T.astype(I32)
     places = iota((16, 128), 0)
     picks = []
@@ -192,9 +204,8 @@
             jnp.where((jnp.broadcast_to(line, (16, 128)) >> 10) == places, 1.0, 0.0)
         )
     pick = jnp.concatenate(picks, axis=0)[:, :64].astype(BF16)
-    cube = cube_q[...]
     for h in range(2):
-        columns = cube[:, h * 8 : h * 8 + 8, :].reshape(64, 384)
+        columns = cube[:, h * 8 : h * 8 + 8, :384].reshape(64, 384)
         chosen = jnp.dot(pick, columns, preferred_element_type=F32).astype(BF16)
         slot_out[:, :, h * 384 : h * 384 + 384] = chosen.reshape(16, 16, 384)
     slot_in[w] = slot_out[w]
@@ -219,7 +230,7 @@
             second_copies.append(copy)
 
     lax.fori_loop(2, 5, decode, 0)
-    loads[2].wait()
+    loads[6].wait()
 
     def to_vectors16(i, _):
         span = pl.ds(pl.multiple_of(i * 128, 128), 128)
@@ -265,17 +276,19 @@
         score_out[p] = jnp.sum(
             jnp.where(iota((16, 128), 1) == places, mine, 0.0), axis=0, keepdims=True
         )
-    score_in[w] = score_out[w]
-    score_copies = []
-    for i in range(1, 16):
-        p, to = plane_peer(i)
-        copy = remote(score_out.at[p], score_in.at[w], rs_s.at[i], rs_r.at[i], to)
-        copy.start()
-        score_copies.append(copy)
+    score_in[me] = score_out[w]
+    offsets = [(dx, dy, dz, dc) for dx in range(4) for dy in range(4) for dz in range(4) for dc in range(2)]
+    offsets.sort(key=lambda o: -sum(min(d, 4 - d) for d in o[:3]))
+    offsets.remove((0, 0, 0, 0))
+    for dx, dy, dz, dc in offsets:
+        p = (y + dy) % 4 * 4 + (z + dz) % 4
+        to = {"group": (x + dx) % 4, "shard": p * 2 + (c + dc) % 2}
+        remote(score_out.at[p], score_in.at[me], rs_s.at[0], rs_r.at[0], to).start()
 
     for copy in core_copies:
         copy.wait_recv()
 
+    loads[5].wait()
     probes = probes_ref[...]
 
     def score_list(l, _):
@@ -288,25 +301,11 @@
         pq_ref[l] = jnp.where(probed > 0.0, sums.T, 0.0)
         return 0
 
-    lax.fori_loop(0, 4, score_list, 0)
-
-    for copy in score_copies:
-        copy.wait_recv()
-    for p in range(16):
-        spread[pl.ds(x * 32 + p * 2 + c, 1), :] = score_in[p]
-    back[a] = spread[...].T[:16, :]
-    back_copies = []
-    for i in range(1, 8):
-        _, to = cube_peer(i)
-        copy = remote(back.at[a], back.at[a], bk_s.at[i], bk_r.at[i], to)
-        copy.start()
-        back_copies.append(copy)
-
-    lax.fori_loop(4, 8, score_list, 0)
-
-    for copy in back_copies:
-        copy.wait_recv()
-    total[...] = jnp.sum(back[...], axis=0)
+    lax.fori_loop(0, 8, score_list, 0)
+
+    everyone = score_in.at[pl.ds(0, 127)]
+    pltpu.make_async_copy(everyone, everyone, rs_r.at[0]).wait()
+    total[...] = score_in[...].reshape(128, 128).T
     own = jnp.where(rank < 0.5, total[pl.ds(a * 2, 1), :], total[pl.ds(a * 2 + 1, 1), :])
     result = jnp.zeros((8, 16), F32)
     for k in range(16):
@@ -317,25 +316,43 @@
     rr_ref[...] = result
 
     for copy in (
-        cube_copies + first_copies + second_copies + core_copies
-        + slot_copies + score_copies + back_copies
+        cube_copies + first_copies + second_copies + core_copies + slot_copies
     ):
         copy.wait_send()
+    pltpu.make_async_copy(everyone, everyone, rs_s.at[0]).wait()
+
+
+def hand_over(pq_in, rr_in, pq_ref, rr_ref, pq, rr, sems):
+    moves = [(rr_in, rr, rr_ref)] + [(pq_in.at[i], pq.at[i], pq_ref.at[i]) for i in range(8)]
+    ins = [pltpu.make_async_copy(a, b, sems.at[0, i]) for i, (a, b, _) in enumerate(moves)]
+    outs = [pltpu.make_async_copy(b, c, sems.at[1, i]) for i, (_, b, c) in enumerate(moves)]
+    for copy in ins:
+        copy.start()
+    for copy_in, copy_out in zip(ins, outs):
+        copy_in.wait()
+        copy_out.start()
+    for copy in outs:
+        copy.wait()
 
 
 def per_device(queries, codebook, pq_codes, probes, vectors, cand_owner, cand_row):
     vmem = pl.BlockSpec(memory_space=pltpu.VMEM)
-    hbm = pl.BlockSpec(memory_space=pl.ANY)
+    hbm = pl.BlockSpec(memory_space=pltpu.HBM)
     dma = pltpu.SemaphoreType.DMA
-    return pl.pallas_call(
+    outs = (
+        jax.ShapeDtypeStruct((8, 256, 256), F32),
+        jax.ShapeDtypeStruct((8, 16), F32),
+    )
+    held = pl.pallas_call(
         kernel,
-        out_shape=(
-            jax.ShapeDtypeStruct((8, 256, 256), F32),
-            jax.ShapeDtypeStruct((8, 16), F32),
-        ),
-        in_specs=[vmem] * 4 + [hbm] * 3,
+        out_shape=outs,
+        in_specs=[hbm] * 7,
         out_specs=(vmem, vmem),
         scratch_shapes=[
+            pltpu.VMEM((8, 768), F32),
+            pltpu.VMEM((8, 256), I32),
+            pltpu.VMEM((8, 16), I32),
+            pltpu.VMEM((8, 16), I32),
             pltpu.VMEM((8, 96, 256), I32),
             pltpu.VMEM((96, 8, 256), F32),
             pltpu.VMEM((1024, 768), F32),
@@ -343,26 +360,23 @@
             pltpu.VMEM((1024, 768), BF16),
             pltpu.VMEM((8, 768, 256), BF16),
             pltpu.VMEM((2, 4, 4, 2, 16, 384), BF16),
-            pltpu.VMEM((8, 16, 384), BF16),
-            pltpu.VMEM((8, 8, 128), F32),
+            pltpu.VMEM((8, 16, 512), BF16),
             pltpu.VMEM((128, 128), I32),
             pltpu.VMEM((16, 1, 128), I32),
             pltpu.VMEM((16, 1, 128), I32),
             pltpu.VMEM((16, 16, 768), BF16),
             pltpu.VMEM((16, 16, 768), BF16),
             pltpu.VMEM((16, 1, 128), F32),
-            pltpu.VMEM((16, 1, 128), F32),
+            pltpu.VMEM((128, 1, 128), F32),
             pltpu.VMEM((128, 128), F32),
-            pltpu.VMEM((8, 16, 128), F32),
-            pltpu.VMEM((16, 128), F32),
-            dma((3,)),
-            dma((8,)), dma((8,)), dma((8,)), dma((8,)),
+            dma((7,)),
+            dma((8,)), dma((8,)),
             dma((2, 3, 4)), dma((2, 3, 4)),
             dma((16,)), dma((16,)), dma((16,)), dma((16,)),
-            dma((16,)), dma((16,)), dma((8,)), dma((8,)),
+            dma((1,)), dma((1,)),
         ],
         compiler_params=pltpu.CompilerParams(
-            vmem_limit_bytes=48 << 20, collective_id=0, has_side_effects=True
+            vmem_limit_bytes=63 << 20, collective_id=0, has_side_effects=True
         ),
         cost_estimate=pl.CostEstimate(flops=3_000_000_000, bytes_accessed=7_000_000, transcendentals=0),
         name="search",
@@ -375,6 +389,15 @@
         codebook.transpose(0, 2, 1),
         vectors,
     )
+    return pl.pallas_call(
+        hand_over,
+        out_shape=outs,
+        in_specs=[hbm] * 2,
+        out_specs=(hbm, hbm),
+        scratch_shapes=[pltpu.VMEM((8, 256, 256), F32), pltpu.VMEM((8, 16), F32), dma((2, 9))],
+        compiler_params=pltpu.CompilerParams(vmem_limit_bytes=63 << 20),
+        name="hand_over",
+    )(*held)
 
 
 def solution(mesh):

time: 42.8 us -> 36.2 us (0.85)
  local copies, waits for them, and re-layouts: 6.98 us -> 0 us
  Pallas kernels: 34.8 us -> 35.4 us
    unnamed x14 -> x0, local copies, waits for them, and re-layouts: 6.98 us -> none
    pallas_call x1 -> x2, Pallas kernels: 34.8 us -> 35.4 us  [the longest x1 33 us: per_device(): pl.pallas_call(kernel, out_shape=outs, in_specs=[hbm] * 7, out_specs=(vme...]
where the time goes in v2:
time: 36.2 us; the launch traced here: 36.1 us
  Pallas kernels  35.4 us (98%)
  between operations  0.64 us (2%)
    pallas_call x1, Pallas kernels, per_device(): pl.pallas_call(kernel, out_shape=outs, in_specs=[hbm] * 7, out_specs=(vme...  33 us
    pallas_call x1, Pallas kernels, per_device(): pl.pallas_call(hand_over, out_shape=outs, in_specs=[hbm] * 2, out_specs=(...  2.42 us

profile of v2, /device:TPU:1, one launch (start us, length us, event | category | flops | bytes accessed | tf_op | source)
XLA Modules:
  0.0 36.1 jit_solution(3370524840669039282)
XLA Ops:
  0.6 33.0 %search.1 = (f32[8,256,256]{2,1,0:T(8,128)}, f32[8,16]{1,0:T(8,128)}) custom-call(f32[8,768]{1,0:T(8,128)} %q_hbm.1, s32[8,256]{1,0:T(8,128)} %bitcast.3, s32[8,16]{1,0:T(8,128)} %owner_hbm.1, s32[8,16]{1,0:T(8,128)} %row_hbm.1, s32[8,96,256]{2,1,0:T(8,128)} %codes_hbm.1, f32[96,8,256]{2,1,0:T(8,128)} %bitcast.2, f32[1024,768]{1,0:T(8,128)} %vectors_hbm.1), custom_call_target="tpu_custom_call" | custom-call | flops 3000000000 | bytes 7000000 | tf_op jit(solution)/shard_map/search/pallas_call | solution.py:346
  33.6 2.4 %hand_over.1 = (f32[8,256,256]{2,1,0:T(8,128)}, f32[8,16]{1,0:T(8,128)}) custom-call(f32[8,256,256]{2,1,0:T(8,128)} %get-tuple-element.4.pq_in, f32[8,16]{1,0:T(8,128)} %get-tuple-element.5.rr_in), custom_call_target="tpu_custom_call" | custom-call | tf_op jit(solution)/shard_map/hand_over/pallas_call | solution.py:392

commit v3 on v2

--- a/solution.py
+++ b/solution.py
@@ -57,6 +57,7 @@
     score_in,
     total,
     load_sem,
+    plane_sem,
     cq_s, cq_r,
     g_s, g_r,
     sq_s, sq_r, sw_s, sw_r,
@@ -79,6 +80,18 @@
     def plane_peer(i):
         p = (w + i) % 16
         return p, device(x, p // 4, p % 4, c)
+
+    def line_peer(axis, i):
+        return (
+            device(x, (y + i) % 4, z, c) if axis == 0 else device(x, y, (z + i) % 4, c)
+        )
+
+    barrier = pltpu.get_barrier_semaphore()
+    for i in (2, 1, 3):
+        for axis in range(2):
+            pl.semaphore_signal(barrier, inc=1, device_id=line_peer(axis, i), device_id_type=MESH)
+    for i in (4, 5, 2, 3, 6, 7, 1):
+        pl.semaphore_signal(barrier, inc=1, device_id=cube_peer(i)[1], device_id_type=MESH)
 
     loads = [
         pltpu.make_async_copy(src, dst, load_sem.at[i])
@@ -96,12 +109,6 @@
     ]
     for load in loads:
         load.start()
-
-    barrier = pltpu.get_barrier_semaphore()
-    for i in range(1, 8):
-        pl.semaphore_signal(barrier, inc=1, device_id=cube_peer(i)[1], device_id_type=MESH)
-    for i in range(1, 16):
-        pl.semaphore_signal(barrier, inc=1, device_id=plane_peer(i)[1], device_id_type=MESH)
 
     def remote(src, dst, send, recv, to):
         return pltpu.make_async_remote_copy(
@@ -135,7 +142,7 @@
         [jnp.where(present > 0.0, slot * 8.0 + upper, -1.0), wanted - upper * 128.0], axis=0
     ).astype(BF16)
 
-    pl.semaphore_wait(barrier, 22)
+    pl.semaphore_wait(barrier, 13)
 
     cube_copies = []
     for i in range(1, 8):
@@ -144,10 +151,8 @@
         copy.start()
         cube_copies.append(copy)
 
-    def line_peer(axis, i):
-        return (
-            device(x, (y + i) % 4, z, c) if axis == 0 else device(x, y, (z + i) % 4, c)
-        )
+    for i in (2, 1, 3):
+        pl.semaphore_signal(plane_sem, inc=1, device_id=line_peer(1, i), device_id_type=MESH)
 
     first_copies, second_copies = [], []
     for i in (1, 3, 2):
@@ -186,10 +191,19 @@
                 )
         return 0
 
-    lax.fori_loop(0, 2, decode, 0)
+    lax.fori_loop(0, 6, decode, 0)
 
     for copy in cube_copies:
         copy.wait_recv()
+    for copy in first_copies:
+        copy.wait_recv()
+    for i in (1, 3, 2):
+        for h in range(2):
+            block = group_q.at[h, :, z, c] if h == 0 else group_q.at[h, y, :, c]
+            copy = remote(block, block, g_s.at[h, 1, i], g_r.at[h, 1, i], line_peer(1 - h, i))
+            copy.start()
+            second_copies.append(copy)
+    pl.semaphore_wait(plane_sem, 3)
     cube = cube_q[...]
     digits = cube[:, :, 384:].astype(F32)
     wants = (digits[:, :8] * 128.0 + digits[:, 8:]).reshape(64, 128)
@@ -220,16 +234,7 @@
             copy.start()
             slot_copies.append(copy)
 
-    for copy in first_copies:
-        copy.wait_recv()
-    for i in (1, 3, 2):
-        for h in range(2):
-            block = group_q.at[h, :, z, c] if h == 0 else group_q.at[h, y, :, c]
-            copy = remote(block, block, g_s.at[h, 1, i], g_r.at[h, 1, i], line_peer(1 - h, i))
-            copy.start()
-            second_copies.append(copy)
-
-    lax.fori_loop(2, 5, decode, 0)
+    lax.fori_loop(6, 8, decode, 0)
     loads[6].wait()
 
     def to_vectors16(i, _):
@@ -248,8 +253,6 @@
         copy = remote(block, block, g_s.at[h, 2, 0], g_r.at[h, 2, 0], sibling)
         copy.start()
         core_copies.append(copy)
-
-    lax.fori_loop(5, 8, decode, 0)
 
     for copy in slot_copies:
         copy.wait_recv()
@@ -322,16 +325,12 @@
     pltpu.make_async_copy(everyone, everyone, rs_s.at[0]).wait()
 
 
-def hand_over(pq_in, rr_in, pq_ref, rr_ref, pq, rr, sems):
-    moves = [(rr_in, rr, rr_ref)] + [(pq_in.at[i], pq.at[i], pq_ref.at[i]) for i in range(8)]
-    ins = [pltpu.make_async_copy(a, b, sems.at[0, i]) for i, (a, b, _) in enumerate(moves)]
-    outs = [pltpu.make_async_copy(b, c, sems.at[1, i]) for i, (_, b, c) in enumerate(moves)]
-    for copy in ins:
+def hand_over(pq_in, rr_in, pq_ref, rr_ref, sems):
+    copies = [pltpu.make_async_copy(rr_in, rr_ref, sems.at[8])]
+    copies += [pltpu.make_async_copy(pq_in.at[i], pq_ref.at[i], sems.at[i]) for i in range(8)]
+    for copy in copies:
         copy.start()
-    for copy_in, copy_out in zip(ins, outs):
-        copy_in.wait()
-        copy_out.start()
-    for copy in outs:
+    for copy in copies:
         copy.wait()
 
 
@@ -370,32 +369,38 @@
             pltpu.VMEM((128, 1, 128), F32),
             pltpu.VMEM((128, 128), F32),
             dma((7,)),
+            pltpu.SemaphoreType.REGULAR,
             dma((8,)), dma((8,)),
             dma((2, 3, 4)), dma((2, 3, 4)),
             dma((16,)), dma((16,)), dma((16,)), dma((16,)),
             dma((1,)), dma((1,)),
         ],
         compiler_params=pltpu.CompilerParams(
-            vmem_limit_bytes=63 << 20, collective_id=0, has_side_effects=True
+            vmem_limit_bytes=32 << 20, collective_id=0, has_side_effects=True
         ),
         cost_estimate=pl.CostEstimate(flops=3_000_000_000, bytes_accessed=7_000_000, transcendentals=0),
         name="search",
     )(
-        queries,
-        probes.T,
-        cand_owner,
-        cand_row,
-        pq_codes,
-        codebook.transpose(0, 2, 1),
-        vectors,
+        *(
+            pltpu.with_memory_space_constraint(operand, pltpu.HBM)
+            for operand in (
+                queries,
+                probes.T,
+                cand_owner,
+                cand_row,
+                pq_codes,
+                codebook.transpose(0, 2, 1),
+                vectors,
+            )
+        )
     )
     return pl.pallas_call(
         hand_over,
         out_shape=outs,
-        in_specs=[hbm] * 2,
+        in_specs=[pl.BlockSpec(memory_space=pl.ANY)] * 2,
         out_specs=(hbm, hbm),
-        scratch_shapes=[pltpu.VMEM((8, 256, 256), F32), pltpu.VMEM((8, 16), F32), dma((2, 9))],
-        compiler_params=pltpu.CompilerParams(vmem_limit_bytes=63 << 20),
+        scratch_shapes=[dma((9,))],
+        compiler_params=pltpu.CompilerParams(vmem_limit_bytes=16 << 20),
         name="hand_over",
     )(*held)
 

time: 36.2 us -> 31.3 us (0.86)
  Pallas kernels: 35.4 us -> 30.6 us
    pallas_call x1, Pallas kernels: 33 us -> 29.2 us  [per_device(): pl.pallas_call(kernel, out_shape=outs, in_specs=[hbm] * 7, out_specs=(vme...]
    pallas_call x1, Pallas kernels: 2.42 us -> 1.39 us  [per_device(): pl.pallas_call(hand_over, out_shape=outs, in_specs=[pl.BlockSpec(memory_s...]
where the time goes in v3:
time: 31.3 us; the launch traced here: 31.2 us
  Pallas kernels  30.6 us (98%)
  between operations  0.64 us (2%)
    pallas_call x1, Pallas kernels, per_device(): pl.pallas_call(kernel, out_shape=outs, in_specs=[hbm] * 7, out_specs=(vme...  29.2 us
    pallas_call x1, Pallas kernels, per_device(): pl.pallas_call(hand_over, out_shape=outs, in_specs=[pl.BlockSpec(memory_s...  1.39 us

profile of v3, /device:TPU:1, one launch (start us, length us, event | category | flops | bytes accessed | tf_op | source)
XLA Modules:
  0.0 31.2 jit_solution(1755167162556964985)
XLA Ops:
  0.6 29.2 %search.1 = (f32[8,256,256]{2,1,0:T(8,128)S(1)}, f32[8,16]{1,0:T(8,128)S(1)}) custom-call(f32[8,768]{1,0:T(8,128)} %q_hbm.1, s32[8,256]{1,0:T(8,128)} %bitcast.3, s32[8,16]{1,0:T(8,128)} %owner_hbm.1, s32[8,16]{1,0:T(8,128)} %row_hbm.1, s32[8,96,256]{2,1,0:T(8,128)} %codes_hbm.1, f32[96,8,256]{2,1,0:T(8,128)} %bitcast.2, f32[1024,768]{1,0:T(8,128)} %vectors_hbm.1), custom_call_target="tpu_custom_call" | custom-call | flops 3000000000 | bytes 7000000 | tf_op jit(solution)/shard_map/search/pallas_call | solution.py:345
  29.8 1.4 %hand_over.1 = (f32[8,256,256]{2,1,0:T(8,128)}, f32[8,16]{1,0:T(8,128)}) custom-call(f32[8,256,256]{2,1,0:T(8,128)S(1)} %get-tuple-element.4.pq_in, f32[8,16]{1,0:T(8,128)S(1)} %get-tuple-element.5.rr_in), custom_call_target="tpu_custom_call" | custom-call | tf_op jit(solution)/shard_map/hand_over/pallas_call | solution.py:397

commit v4 on v3

--- a/solution.py
+++ b/solution.py
@@ -7,6 +7,7 @@
 
 MESH = pl.DeviceIdType.MESH
 F32, BF16, I32 = jnp.float32, jnp.bfloat16, jnp.int32
+GROUP = 16
 
 
 def lane_gather(table, index):
@@ -48,7 +49,9 @@
     decoded,
     group_q,
     cube_q,
-    want_t,
+    slot_t,
+    place_t,
+    row_t,
     want_out,
     want_in,
     slot_out,
@@ -77,9 +80,12 @@
         p = (a + i) % 8
         return p, device(p // 2, y, z, p % 2)
 
-    def plane_peer(i):
-        p = (w + i) % 16
-        return p, device(x, p // 4, p % 4, c)
+    def plane_peer(dy, dz):
+        to_y, to_z = (y + dy) % 4, (z + dz) % 4
+        return to_y * 4 + to_z, device(x, to_y, to_z, c)
+
+    plane_offsets = [(dy, dz) for dy in range(4) for dz in range(4)]
+    plane_offsets.sort(key=lambda o: -sum(min(d, 4 - d) for d in o))
 
     def line_peer(axis, i):
         return (
@@ -137,10 +143,17 @@
     earlier = (iota((8, 8), 1) < iota((8, 8), 0)).astype(BF16)
     rank = jnp.dot(earlier, present.astype(BF16), preferred_element_type=F32)
     slot = (a * 2).astype(F32) + rank
-    upper = jnp.floor(wanted * (1.0 / 128.0))
+    rows = [
+        jnp.sum(jnp.where((present > 0.0) & (rank == float(k)), wanted, 0.0), axis=0, keepdims=True)
+        for k in range(2)
+    ]
+    rows = jnp.concatenate(rows + [jnp.zeros((6, 128), F32)], axis=0)
+    upper = jnp.floor(rows * (1.0 / 32.0))
+    digits = upper + pltpu.roll(rows - upper * 32.0, 2, 0)
     cube_q[a, :, 384:] = jnp.concatenate(
-        [jnp.where(present > 0.0, slot * 8.0 + upper, -1.0), wanted - upper * 128.0], axis=0
+        [jnp.where(present > 0.0, slot, -1.0), digits], axis=0
     ).astype(BF16)
+    place_t[...] = jnp.zeros((128, 128), F32)
 
     pl.semaphore_wait(barrier, 13)
 
@@ -195,6 +208,50 @@
 
     for copy in cube_copies:
         copy.wait_recv()
+    pl.semaphore_wait(plane_sem, 3)
+    cube = cube_q[...]
+    codes_in = cube[:, :, 384:].astype(F32)
+    slot_t[...] = jnp.concatenate(
+        [codes_in[:, :8].reshape(64, 128), jnp.full((64, 128), -1.0, F32)], axis=0
+    ).T
+    for k in range(8):
+        pair = codes_in[k, 8:10] * 32.0 + codes_in[k, 10:12]
+        place_t[pl.ds(pl.multiple_of(w % 8 * 16, 16), 16), :] += jnp.pad(
+            pair, ((2 * k, 14 - 2 * k), (0, 0))
+        )
+    row_t[...] = place_t[...].T
+    columns = [cube[:, h * 8 : h * 8 + 8, :384].reshape(64, 384) for h in range(2)]
+    columns = jnp.concatenate(columns, axis=1)
+    places = iota((16, 128), 0).astype(F32)
+    slot_copies = []
+    for first in range(0, 16, GROUP):
+        group = plane_offsets[first : first + GROUP]
+        picks = []
+        for dy, dz in group:
+            p, _ = plane_peer(dy, dz)
+            line = pl.ds(x * 32 + p * 2 + c, 1)
+            want_out[dy * 4 + dz] = row_t[line, :]
+            picks.append(
+                jnp.where(jnp.broadcast_to(slot_t[line, :], (16, 128)) == places, 1.0, 0.0)
+            )
+        pick = jnp.concatenate(picks, axis=0)[:, :64].astype(BF16)
+        chosen = jnp.dot(pick, columns, preferred_element_type=F32).astype(BF16)
+        for n, (dy, dz) in enumerate(group):
+            k = dy * 4 + dz
+            if k == 0:
+                slot_in[w] = chosen[n * 16 : n * 16 + 16]
+                want_in[w] = want_out[0]
+                continue
+            slot_out[k] = chosen[n * 16 : n * 16 + 16]
+            _, to = plane_peer(dy, dz)
+            for copy in (
+                remote(want_out.at[k], want_in.at[w], sw_s.at[k], sw_r.at[k], to),
+                remote(slot_out.at[k], slot_in.at[w], sq_s.at[k], sq_r.at[k], to),
+            ):
+                copy.start()
+                slot_copies.append(copy)
+
+    lax.fori_loop(6, 8, decode, 0)
     for copy in first_copies:
         copy.wait_recv()
     for i in (1, 3, 2):
@@ -203,38 +260,6 @@
             copy = remote(block, block, g_s.at[h, 1, i], g_r.at[h, 1, i], line_peer(1 - h, i))
             copy.start()
             second_copies.append(copy)
-    pl.semaphore_wait(plane_sem, 3)
-    cube = cube_q[...]
-    digits = cube[:, :, 384:].astype(F32)
-    wants = (digits[:, :8] * 128.0 + digits[:, 8:]).reshape(64, 128)
-    wants = jnp.concatenate([wants, jnp.full((64, 128), -1.0, F32)], axis=0)
-    want_t[...] = wants.T.astype(I32)
-    places = iota((16, 128), 0)
-    picks = []
-    for p in range(16):
-        line = want_t[pl.ds(x * 32 + p * 2 + c, 1), :]
-        want_out[p] = line
-        picks.append(
-            jnp.where((jnp.broadcast_to(line, (16, 128)) >> 10) == places, 1.0, 0.0)
-        )
-    pick = jnp.concatenate(picks, axis=0)[:, :64].astype(BF16)
-    for h in range(2):
-        columns = cube[:, h * 8 : h * 8 + 8, :384].reshape(64, 384)
-        chosen = jnp.dot(pick, columns, preferred_element_type=F32).astype(BF16)
-        slot_out[:, :, h * 384 : h * 384 + 384] = chosen.reshape(16, 16, 384)
-    slot_in[w] = slot_out[w]
-    want_in[w] = want_out[w]
-    slot_copies = []
-    for i in range(1, 16):
-        p, to = plane_peer(i)
-        for copy in (
-            remote(slot_out.at[p], slot_in.at[w], sq_s.at[i], sq_r.at[i], to),
-            remote(want_out.at[p], want_in.at[w], sw_s.at[i], sw_r.at[i], to),
-        ):
-            copy.start()
-            slot_copies.append(copy)
-
-    lax.fori_loop(6, 8, decode, 0)
     loads[6].wait()
 
     def to_vectors16(i, _):
@@ -243,6 +268,33 @@
         return 0
 
     lax.fori_loop(0, 8, to_vectors16, 0)
+
+    for copy in slot_copies:
+        copy.wait_recv()
+    slots = slot_in[...].reshape(256, 768)
+    ids = jnp.concatenate(
+        [jnp.sum(want_in[b * 8 : b * 8 + 8], axis=0) for b in range(2)], axis=1
+    ).astype(I32)
+    found = jnp.zeros((256, 256), F32)
+    for b in range(4):
+        part = lax.dot_general(
+            vectors16[b * 256 : b * 256 + 256, :],
+            slots,
+            (((1,), (1,)), ((), ())),
+            preferred_element_type=F32,
+        )
+        found = jnp.where(iota((256, 256), 0) + b * 256 == ids, part, found)
+    scored = jnp.sum(found, axis=0, keepdims=True)
+    for b in range(2):
+        score_out[b] = scored[:, b * 128 : b * 128 + 128]
+    score_in[me] = score_out[w // 8]
+    offsets = [(dx, dy, dz, dc) for dx in range(4) for dy in range(4) for dz in range(4) for dc in range(2)]
+    offsets.sort(key=lambda o: -sum(min(d, 4 - d) for d in o[:3]))
+    offsets.remove((0, 0, 0, 0))
+    for dx, dy, dz, dc in offsets:
+        p = (y + dy) % 4 * 4 + (z + dz) % 4
+        to = {"group": (x + dx) % 4, "shard": p * 2 + (c + dc) % 2}
+        remote(score_out.at[p // 8], score_in.at[me], rs_s.at[0], rs_r.at[0], to).start()
 
     for copy in second_copies:
         copy.wait_recv()
@@ -253,41 +305,6 @@
         copy = remote(block, block, g_s.at[h, 2, 0], g_r.at[h, 2, 0], sibling)
         copy.start()
         core_copies.append(copy)
-
-    for copy in slot_copies:
-        copy.wait_recv()
-    slots = slot_in[...].reshape(256, 768)
-    ids = []
-    for p in range(16):
-        line = jnp.broadcast_to(want_in[p], (16, 128))
-        ids.append(jnp.where((line >> 10) == places, line & 1023, 0))
-    ids = jnp.sum(jnp.concatenate(ids, axis=0).astype(F32), axis=1, keepdims=True).astype(I32)
-    found = jnp.zeros((256, 256), F32)
-    for b in range(4):
-        part = lax.dot_general(
-            slots,
-            vectors16[b * 256 : b * 256 + 256, :],
-            (((1,), (1,)), ((), ())),
-            preferred_element_type=F32,
-        )
-        found = jnp.where(iota((256, 256), 1) + b * 256 == ids, part, found)
-        if b == 0:
-            found = jnp.where(iota((256, 256), 1) == ids, part, 0.0)
-    scored = jnp.sum(found, axis=1, keepdims=True)
-    for p in range(16):
-        mine = jnp.broadcast_to(scored[p * 16 : p * 16 + 16, :], (16, 128))
-        score_out[p] = jnp.sum(
-            jnp.where(iota((16, 128), 1) == places, mine, 0.0), axis=0, keepdims=True
-        )
-    score_in[me] = score_out[w]
-    offsets = [(dx, dy, dz, dc) for dx in range(4) for dy in range(4) for dz in range(4) for dc in range(2)]
-    offsets.sort(key=lambda o: -sum(min(d, 4 - d) for d in o[:3]))
-    offsets.remove((0, 0, 0, 0))
-    for dx, dy, dz, dc in offsets:
-        p = (y + dy) % 4 * 4 + (z + dz) % 4
-        to = {"group": (x + dx) % 4, "shard": p * 2 + (c + dc) % 2}
-        remote(score_out.at[p], score_in.at[me], rs_s.at[0], rs_r.at[0], to).start()
-
     for copy in core_copies:
         copy.wait_recv()
 
@@ -309,7 +326,8 @@
     everyone = score_in.at[pl.ds(0, 127)]
     pltpu.make_async_copy(everyone, everyone, rs_r.at[0]).wait()
     total[...] = score_in[...].reshape(128, 128).T
-    own = jnp.where(rank < 0.5, total[pl.ds(a * 2, 1), :], total[pl.ds(a * 2 + 1, 1), :])
+    line = w % 8 * 16 + a * 2
+    own = jnp.where(rank < 0.5, total[pl.ds(line, 1), :], total[pl.ds(line + 1, 1), :])
     result = jnp.zeros((8, 16), F32)
     for k in range(16):
         value = jnp.sum(
@@ -360,12 +378,14 @@
             pltpu.VMEM((8, 768, 256), BF16),
             pltpu.VMEM((2, 4, 4, 2, 16, 384), BF16),
             pltpu.VMEM((8, 16, 512), BF16),
-            pltpu.VMEM((128, 128), I32),
-            pltpu.VMEM((16, 1, 128), I32),
-            pltpu.VMEM((16, 1, 128), I32),
+            pltpu.VMEM((128, 128), F32),
+            pltpu.VMEM((128, 128), F32),
+            pltpu.VMEM((128, 128), F32),
+            pltpu.VMEM((16, 1, 128), F32),
+            pltpu.VMEM((16, 1, 128), F32),
             pltpu.VMEM((16, 16, 768), BF16),
             pltpu.VMEM((16, 16, 768), BF16),
-            pltpu.VMEM((16, 1, 128), F32),
+            pltpu.VMEM((2, 1, 128), F32),
             pltpu.VMEM((128, 1, 128), F32),
             pltpu.VMEM((128, 128), F32),
             dma((7,)),

time: 31.3 us -> 30.1 us (0.962)
  Pallas kernels: 30.6 us -> 29.3 us
    pallas_call x1, Pallas kernels: 29.2 us -> 27.9 us  [per_device(): pl.pallas_call(kernel, out_shape=outs, in_specs=[hbm] * 7, out_specs=(vme...]
where the time goes in v4:
time: 30.1 us; the launch traced here: 30 us
  Pallas kernels  29.3 us (97%)
  between operations  0.64 us (2%)
    pallas_call x1, Pallas kernels, per_device(): pl.pallas_call(kernel, out_shape=outs, in_specs=[hbm] * 7, out_specs=(vme...  27.9 us
    pallas_call x1, Pallas kernels, per_device(): pl.pallas_call(hand_over, out_shape=outs, in_specs=[pl.BlockSpec(memory_s...  1.39 us

profile of v4, /device:TPU:1, one launch (start us, length us, event | category | flops | bytes accessed | tf_op | source)
XLA Modules:
  0.0 30.0 jit_solution(6087160049955607446)
XLA Ops:
  0.6 27.9 %search.1 = (f32[8,256,256]{2,1,0:T(8,128)S(1)}, f32[8,16]{1,0:T(8,128)S(1)}) custom-call(f32[8,768]{1,0:T(8,128)} %q_hbm.1, s32[8,256]{1,0:T(8,128)} %bitcast.3, s32[8,16]{1,0:T(8,128)} %owner_hbm.1, s32[8,16]{1,0:T(8,128)} %row_hbm.1, s32[8,96,256]{2,1,0:T(8,128)} %codes_hbm.1, f32[96,8,256]{2,1,0:T(8,128)} %bitcast.2, f32[1024,768]{1,0:T(8,128)} %vectors_hbm.1), custom_call_target="tpu_custom_call" | custom-call | flops 3000000000 | bytes 7000000 | tf_op jit(solution)/shard_map/search/pallas_call | solution.py:363
  28.6 1.4 %hand_over.1 = (f32[8,256,256]{2,1,0:T(8,128)}, f32[8,16]{1,0:T(8,128)}) custom-call(f32[8,256,256]{2,1,0:T(8,128)S(1)} %get-tuple-element.4.pq_in, f32[8,16]{1,0:T(8,128)S(1)} %get-tuple-element.5.rr_in), custom_call_target="tpu_custom_call" | custom-call | tf_op jit(solution)/shard_map/hand_over/pallas_call | solution.py:417

commit v5 on v4

--- a/solution.py
+++ b/solution.py
@@ -321,7 +321,7 @@
         pq_ref[l] = jnp.where(probed > 0.0, sums.T, 0.0)
         return 0
 
-    lax.fori_loop(0, 8, score_list, 0)
+    lax.fori_loop(0, 8, score_list, 0, unroll=2)
 
     everyone = score_in.at[pl.ds(0, 127)]
     pltpu.make_async_copy(everyone, everyone, rs_r.at[0]).wait()

time: 30.1 us -> 29.5 us (0.980)
  Pallas kernels: 29.3 us -> 28.7 us
    pallas_call x1, Pallas kernels: 27.9 us -> 27.3 us  [per_device(): pl.pallas_call(kernel, out_shape=outs, in_specs=[hbm] * 7, out_specs=(vme...]
where the time goes in v5:
time: 29.5 us; the launch traced here: 29.4 us
  Pallas kernels  28.7 us (97%)
  between operations  0.64 us (2%)
    pallas_call x1, Pallas kernels, per_device(): pl.pallas_call(kernel, out_shape=outs, in_specs=[hbm] * 7, out_specs=(vme...  27.3 us
    pallas_call x1, Pallas kernels, per_device(): pl.pallas_call(hand_over, out_shape=outs, in_specs=[pl.BlockSpec(memory_s...  1.39 us

profile of v5, /device:TPU:1, one launch (start us, length us, event | category | flops | bytes accessed | tf_op | source)
XLA Modules:
  0.0 29.4 jit_solution(10527229511522042467)
XLA Ops:
  0.6 27.3 %search.1 = (f32[8,256,256]{2,1,0:T(8,128)S(1)}, f32[8,16]{1,0:T(8,128)S(1)}) custom-call(f32[8,768]{1,0:T(8,128)} %q_hbm.1, s32[8,256]{1,0:T(8,128)} %bitcast.3, s32[8,16]{1,0:T(8,128)} %owner_hbm.1, s32[8,16]{1,0:T(8,128)} %row_hbm.1, s32[8,96,256]{2,1,0:T(8,128)} %codes_hbm.1, f32[96,8,256]{2,1,0:T(8,128)} %bitcast.2, f32[1024,768]{1,0:T(8,128)} %vectors_hbm.1), custom_call_target="tpu_custom_call" | custom-call | flops 3000000000 | bytes 7000000 | tf_op jit(solution)/shard_map/search/pallas_call | solution.py:363
  28.0 1.4 %hand_over.1 = (f32[8,256,256]{2,1,0:T(8,128)}, f32[8,16]{1,0:T(8,128)}) custom-call(f32[8,256,256]{2,1,0:T(8,128)S(1)} %get-tuple-element.4.pq_in, f32[8,16]{1,0:T(8,128)S(1)} %get-tuple-element.5.rr_in), custom_call_target="tpu_custom_call" | custom-call | tf_op jit(solution)/shard_map/hand_over/pallas_call | solution.py:417

commit v6 on v5

--- a/solution.py
+++ b/solution.py
@@ -158,7 +158,7 @@
     pl.semaphore_wait(barrier, 13)
 
     cube_copies = []
-    for i in range(1, 8):
+    for i in (4, 5, 3, 2, 6, 7, 1):
         _, to = cube_peer(i)
         copy = remote(cube_q.at[a], cube_q.at[a], cq_s.at[i], cq_r.at[i], to)
         copy.start()
@@ -220,17 +220,26 @@
             pair, ((2 * k, 14 - 2 * k), (0, 0))
         )
     row_t[...] = place_t[...].T
+    slot_copies = []
+    for dy, dz in plane_offsets:
+        k = dy * 4 + dz
+        p, to = plane_peer(dy, dz)
+        want_out[k] = row_t[pl.ds(x * 32 + p * 2 + c, 1), :]
+        if k == 0:
+            want_in[w] = want_out[0]
+            continue
+        copy = remote(want_out.at[k], want_in.at[w], sw_s.at[k], sw_r.at[k], to)
+        copy.start()
+        slot_copies.append(copy)
     columns = [cube[:, h * 8 : h * 8 + 8, :384].reshape(64, 384) for h in range(2)]
     columns = jnp.concatenate(columns, axis=1)
     places = iota((16, 128), 0).astype(F32)
-    slot_copies = []
     for first in range(0, 16, GROUP):
         group = plane_offsets[first : first + GROUP]
         picks = []
         for dy, dz in group:
             p, _ = plane_peer(dy, dz)
             line = pl.ds(x * 32 + p * 2 + c, 1)
-            want_out[dy * 4 + dz] = row_t[line, :]
             picks.append(
                 jnp.where(jnp.broadcast_to(slot_t[line, :], (16, 128)) == places, 1.0, 0.0)
             )
@@ -240,16 +249,12 @@
             k = dy * 4 + dz
             if k == 0:
                 slot_in[w] = chosen[n * 16 : n * 16 + 16]
-                want_in[w] = want_out[0]
                 continue
             slot_out[k] = chosen[n * 16 : n * 16 + 16]
             _, to = plane_peer(dy, dz)
-            for copy in (
-                remote(want_out.at[k], want_in.at[w], sw_s.at[k], sw_r.at[k], to),
-                remote(slot_out.at[k], slot_in.at[w], sq_s.at[k], sq_r.at[k], to),
-            ):
-                copy.start()
-                slot_copies.append(copy)
+            copy = remote(slot_out.at[k], slot_in.at[w], sq_s.at[k], sq_r.at[k], to)
+            copy.start()
+            slot_copies.append(copy)
 
     lax.fori_loop(6, 8, decode, 0)
     for copy in first_copies:

time: 29.5 us -> 29.2 us (0.990)
  Pallas kernels: 28.7 us -> 28.4 us
    pallas_call x1, Pallas kernels: 27.3 us -> 27 us  [per_device(): pl.pallas_call(kernel, out_shape=outs, in_specs=[hbm] * 7, out_specs=(vme...]
where the time goes in v6:
time: 29.2 us; the launch traced here: 29 us
  Pallas kernels  28.4 us (97%)
  between operations  0.64 us (2%)
    pallas_call x1, Pallas kernels, per_device(): pl.pallas_call(kernel, out_shape=outs, in_specs=[hbm] * 7, out_specs=(vme...  27 us
    pallas_call x1, Pallas kernels, per_device(): pl.pallas_call(hand_over, out_shape=outs, in_specs=[pl.BlockSpec(memory_s...  1.39 us

profile of v6, /device:TPU:1, one launch (start us, length us, event | category | flops | bytes accessed | tf_op | source)
XLA Modules:
  0.0 29.0 jit_solution(15317637448008960961)
XLA Ops:
  0.6 27.0 %search.1 = (f32[8,256,256]{2,1,0:T(8,128)S(1)}, f32[8,16]{1,0:T(8,128)S(1)}) custom-call(f32[8,768]{1,0:T(8,128)} %q_hbm.1, s32[8,256]{1,0:T(8,128)} %bitcast.3, s32[8,16]{1,0:T(8,128)} %owner_hbm.1, s32[8,16]{1,0:T(8,128)} %row_hbm.1, s32[8,96,256]{2,1,0:T(8,128)} %codes_hbm.1, f32[96,8,256]{2,1,0:T(8,128)} %bitcast.2, f32[1024,768]{1,0:T(8,128)} %vectors_hbm.1), custom_call_target="tpu_custom_call" | custom-call | flops 3000000000 | bytes 7000000 | tf_op jit(solution)/shard_map/search/pallas_call | solution.py:368
  27.7 1.4 %hand_over.1 = (f32[8,256,256]{2,1,0:T(8,128)}, f32[8,16]{1,0:T(8,128)}) custom-call(f32[8,256,256]{2,1,0:T(8,128)S(1)} %get-tuple-element.4.pq_in, f32[8,16]{1,0:T(8,128)S(1)} %get-tuple-element.5.rr_in), custom_call_target="tpu_custom_call" | custom-call | tf_op jit(solution)/shard_map/hand_over/pallas_call | solution.py:422

commit v7 on v6

--- a/solution.py
+++ b/solution.py
@@ -49,6 +49,7 @@
     decoded,
     group_q,
     cube_q,
+    cube_w,
     slot_t,
     place_t,
     row_t,
@@ -61,7 +62,7 @@
     total,
     load_sem,
     plane_sem,
-    cq_s, cq_r,
+    cq_s, cq_r, cw_s, cw_r,
     g_s, g_r,
     sq_s, sq_r, sw_s, sw_r,
     rs_s, rs_r,
@@ -126,7 +127,7 @@
     q = q_ref[...]
     high = q.astype(BF16)
     low = (q - high.astype(F32)).astype(BF16)
-    cube_q[a, :, :384] = jnp.concatenate([high[:, :384], high[:, 384:]], axis=0)
+    cube_q[a] = jnp.concatenate([high[:, :384], high[:, 384:]], axis=0)
     for h in range(2):
         group_q[h, y, z, c] = jnp.concatenate(
             [high[:, h * 384 : h * 384 + 384], low[:, h * 384 : h * 384 + 384]], axis=0
@@ -150,19 +151,22 @@
     rows = jnp.concatenate(rows + [jnp.zeros((6, 128), F32)], axis=0)
     upper = jnp.floor(rows * (1.0 / 32.0))
     digits = upper + pltpu.roll(rows - upper * 32.0, 2, 0)
-    cube_q[a, :, 384:] = jnp.concatenate(
+    cube_w[a] = jnp.concatenate(
         [jnp.where(present > 0.0, slot, -1.0), digits], axis=0
     ).astype(BF16)
     place_t[...] = jnp.zeros((128, 128), F32)
 
     pl.semaphore_wait(barrier, 13)
 
-    cube_copies = []
-    for i in (4, 5, 3, 2, 6, 7, 1):
-        _, to = cube_peer(i)
-        copy = remote(cube_q.at[a], cube_q.at[a], cq_s.at[i], cq_r.at[i], to)
-        copy.start()
-        cube_copies.append(copy)
+    cube_copies, wish_copies = [], []
+    for block, send, recv, copies in (
+        (cube_w.at[a], cw_s, cw_r, wish_copies),
+        (cube_q.at[a], cq_s, cq_r, cube_copies),
+    ):
+        for i in (4, 5, 3, 2, 6, 7, 1):
+            copy = remote(block, block, send.at[i], recv.at[i], cube_peer(i)[1])
+            copy.start()
+            copies.append(copy)
 
     for i in (2, 1, 3):
         pl.semaphore_signal(plane_sem, inc=1, device_id=line_peer(1, i), device_id_type=MESH)
@@ -206,11 +210,10 @@
 
     lax.fori_loop(0, 6, decode, 0)
 
-    for copy in cube_copies:
+    for copy in wish_copies:
         copy.wait_recv()
     pl.semaphore_wait(plane_sem, 3)
-    cube = cube_q[...]
-    codes_in = cube[:, :, 384:].astype(F32)
+    codes_in = cube_w[...].astype(F32)
     slot_t[...] = jnp.concatenate(
         [codes_in[:, :8].reshape(64, 128), jnp.full((64, 128), -1.0, F32)], axis=0
     ).T
@@ -231,19 +234,21 @@
         copy = remote(want_out.at[k], want_in.at[w], sw_s.at[k], sw_r.at[k], to)
         copy.start()
         slot_copies.append(copy)
-    columns = [cube[:, h * 8 : h * 8 + 8, :384].reshape(64, 384) for h in range(2)]
+    places = iota((16, 128), 0).astype(F32)
+    picks = []
+    for dy, dz in plane_offsets:
+        p, _ = plane_peer(dy, dz)
+        line = jnp.broadcast_to(slot_t[pl.ds(x * 32 + p * 2 + c, 1), :], (16, 128))
+        picks.append(jnp.where(line == places, 1.0, 0.0))
+    pick_all = jnp.concatenate(picks, axis=0)[:, :64].astype(BF16)
+    for copy in cube_copies:
+        copy.wait_recv()
+    cube = cube_q[...]
+    columns = [cube[:, h * 8 : h * 8 + 8, :].reshape(64, 384) for h in range(2)]
     columns = jnp.concatenate(columns, axis=1)
-    places = iota((16, 128), 0).astype(F32)
     for first in range(0, 16, GROUP):
         group = plane_offsets[first : first + GROUP]
-        picks = []
-        for dy, dz in group:
-            p, _ = plane_peer(dy, dz)
-            line = pl.ds(x * 32 + p * 2 + c, 1)
-            picks.append(
-                jnp.where(jnp.broadcast_to(slot_t[line, :], (16, 128)) == places, 1.0, 0.0)
-            )
-        pick = jnp.concatenate(picks, axis=0)[:, :64].astype(BF16)
+        pick = pick_all[first * 16 : (first + GROUP) * 16]
         chosen = jnp.dot(pick, columns, preferred_element_type=F32).astype(BF16)
         for n, (dy, dz) in enumerate(group):
             k = dy * 4 + dz
@@ -342,7 +347,7 @@
     rr_ref[...] = result
 
     for copy in (
-        cube_copies + first_copies + second_copies + core_copies + slot_copies
+        wish_copies + cube_copies + first_copies + second_copies + core_copies + slot_copies
     ):
         copy.wait_send()
     pltpu.make_async_copy(everyone, everyone, rs_s.at[0]).wait()
@@ -382,7 +387,8 @@
             pltpu.VMEM((1024, 768), BF16),
             pltpu.VMEM((8, 768, 256), BF16),
             pltpu.VMEM((2, 4, 4, 2, 16, 384), BF16),
-            pltpu.VMEM((8, 16, 512), BF16),
+            pltpu.VMEM((8, 16, 384), BF16),
+            pltpu.VMEM((8, 16, 128), BF16),
             pltpu.VMEM((128, 128), F32),
             pltpu.VMEM((128, 128), F32),
             pltpu.VMEM((128, 128), F32),
@@ -395,7 +401,7 @@
             pltpu.VMEM((128, 128), F32),
             dma((7,)),
             pltpu.SemaphoreType.REGULAR,
-            dma((8,)), dma((8,)),
+            dma((8,)), dma((8,)), dma((8,)), dma((8,)),
             dma((2, 3, 4)), dma((2, 3, 4)),
             dma((16,)), dma((16,)), dma((16,)), dma((16,)),
             dma((1,)), dma((1,)),

time: 29.2 us -> 29.2 us (level)
  no operation moved by 1% of the time
where the time goes in v7:
time: 29.2 us; the launch traced here: 29.1 us
  Pallas kernels  28.4 us (97%)
  between operations  0.64 us (2%)
    pallas_call x1, Pallas kernels, per_device(): pl.pallas_call(kernel, out_shape=outs, in_specs=[hbm] * 7, out_specs=(vme...  27 us
    pallas_call x1, Pallas kernels, per_device(): pl.pallas_call(hand_over, out_shape=outs, in_specs=[pl.BlockSpec(memory_s...  1.39 us

profile of v7, /device:TPU:1, one launch (start us, length us, event | category | flops | bytes accessed | tf_op | source)
XLA Modules:
  0.0 29.1 jit_solution(9377477257879766622)
XLA Ops:
  0.6 27.0 %search.1 = (f32[8,256,256]{2,1,0:T(8,128)S(1)}, f32[8,16]{1,0:T(8,128)S(1)}) custom-call(f32[8,768]{1,0:T(8,128)} %q_hbm.1, s32[8,256]{1,0:T(8,128)} %bitcast.3, s32[8,16]{1,0:T(8,128)} %owner_hbm.1, s32[8,16]{1,0:T(8,128)} %row_hbm.1, s32[8,96,256]{2,1,0:T(8,128)} %codes_hbm.1, f32[96,8,256]{2,1,0:T(8,128)} %bitcast.2, f32[1024,768]{1,0:T(8,128)} %vectors_hbm.1), custom_call_target="tpu_custom_call" | custom-call | flops 3000000000 | bytes 7000000 | tf_op jit(solution)/shard_map/search/pallas_call | solution.py:373
  27.7 1.4 %hand_over.1 = (f32[8,256,256]{2,1,0:T(8,128)}, f32[8,16]{1,0:T(8,128)}) custom-call(f32[8,256,256]{2,1,0:T(8,128)S(1)} %get-tuple-element.4.pq_in, f32[8,16]{1,0:T(8,128)S(1)} %get-tuple-element.5.rr_in), custom_call_target="tpu_custom_call" | custom-call | tf_op jit(solution)/shard_map/hand_over/pallas_call | solution.py:428

commit v8 on v7

--- a/solution.py
+++ b/solution.py
@@ -208,7 +208,7 @@
                 )
         return 0
 
-    lax.fori_loop(0, 6, decode, 0)
+    lax.fori_loop(0, 3, decode, 0)
 
     for copy in wish_copies:
         copy.wait_recv()
@@ -261,7 +261,7 @@
             copy.start()
             slot_copies.append(copy)
 
-    lax.fori_loop(6, 8, decode, 0)
+    lax.fori_loop(3, 8, decode, 0)
     for copy in first_copies:
         copy.wait_recv()
     for i in (1, 3, 2):

time: 29.2 us -> 29.2 us (level)
  no operation moved by 1% of the time
where the time goes in v8:
time: 29.2 us; the launch traced here: 29.1 us
  Pallas kernels  28.4 us (97%)
  between operations  0.64 us (2%)
    pallas_call x1, Pallas kernels, per_device(): pl.pallas_call(kernel, out_shape=outs, in_specs=[hbm] * 7, out_specs=(vme...  27 us
    pallas_call x1, Pallas kernels, per_device(): pl.pallas_call(hand_over, out_shape=outs, in_specs=[pl.BlockSpec(memory_s...  1.39 us

profile of v8, /device:TPU:1, one launch (start us, length us, event | category | flops | bytes accessed | tf_op | source)
XLA Modules:
  0.0 29.1 jit_solution(9537183979815310408)
XLA Ops:
  0.6 27.0 %search.1 = (f32[8,256,256]{2,1,0:T(8,128)S(1)}, f32[8,16]{1,0:T(8,128)S(1)}) custom-call(f32[8,768]{1,0:T(8,128)} %q_hbm.1, s32[8,256]{1,0:T(8,128)} %bitcast.3, s32[8,16]{1,0:T(8,128)} %owner_hbm.1, s32[8,16]{1,0:T(8,128)} %row_hbm.1, s32[8,96,256]{2,1,0:T(8,128)} %codes_hbm.1, f32[96,8,256]{2,1,0:T(8,128)} %bitcast.2, f32[1024,768]{1,0:T(8,128)} %vectors_hbm.1), custom_call_target="tpu_custom_call" | custom-call | flops 3000000000 | bytes 7000000 | tf_op jit(solution)/shard_map/search/pallas_call | solution.py:373
  27.7 1.4 %hand_over.1 = (f32[8,256,256]{2,1,0:T(8,128)}, f32[8,16]{1,0:T(8,128)}) custom-call(f32[8,256,256]{2,1,0:T(8,128)S(1)} %get-tuple-element.4.pq_in, f32[8,16]{1,0:T(8,128)S(1)} %get-tuple-element.5.rr_in), custom_call_target="tpu_custom_call" | custom-call | tf_op jit(solution)/shard_map/hand_over/pallas_call | solution.py:428
